TPU v7x, 128 devices: a whole 4x4x4 slice. The times are simulated.
128 devices in a mesh: frame: 64 (over z, y, x), tile: 2 (over core).
Axes of the slice: x: 4, y: 4, z: 4, core: 2. Of those that a mesh axis runs over, the one named last changes fastest.
Arguments:
- frames_in: bfloat16 [768, 256, 1152], P('frame', 'tile'), may hold values from -10 to 10
- norm_gain: float32 [1152], replicated, may hold values from 0.5 to 1.5
- norm_bias: float32 [1152], replicated, may hold values from -3 to 3
- w_qkv: bfloat16 [1152, 3456], replicated, may hold values from -3.5 to 3.5
- w_out: bfloat16 [1152, 1152], replicated, may hold values from -0.1875 to 0.1875
- time_taps: float32 [3, 1152], replicated, may hold values from 0.25 to 1
- w_proj: bfloat16 [1152, 3584], P(None, 'tile'), may hold values from -0.1875 to 0.1875
- clip_lengths: int32 [6], replicated, may hold values from 1 to 96, 384 in all
- frame_slot: int32 [768], replicated, may hold values from -1 to 383, as said below
- block_map: int32 [64], replicated, may hold values from 0 to 63, each once
Outputs:
- video_tokens: bfloat16 [384, 64, 3584], P('frame', None, 'tile')
Inputs may be any that keep to these rules, and one draw needn't show every extreme that they name: `frame_slot`: each frame 0 to 383 is held by exactly one slot; -1 marks an empty slot; a device's live slots come first among its 12, and some device has all 12 live. `clip_lengths`: the lengths sum to 384; clip 0's frames come first in frame order, then clip 1's, and so on. `block_map`: A permutation.
All inputs are finite; a program needn't handle non-finite values.
Results may differ from a plain program's by a relative error of at most 0.012.
Values may be sent and summed in bfloat16 or wider, within the bound.
No kernel may reach another device: no remote copies, remote signals or barrier semaphores. Data moves between devices by JAX's collectives and lax.ppermute only.
A program may use at most 192 MiB of HBM per device.

v0:
```python
import math

import jax
import jax.numpy as jnp
from jax import lax
from jax.experimental import pallas as pl
from jax.experimental.pallas import tpu as pltpu
from jax.sharding import PartitionSpec as P

D = 1152
HEADS = 16
HEAD_DIM = 72
PATCH = 256
HALF = 128
BLOCKS = 64
FRAMES = 384
FRAME_DEVS = 64
CLIPS = 6
FR_DEV = 6
SLOT_DEV = 12
PAIRS = 3
OUT_DEV = 1792
NORM_EPS = 1e-6
SCORE_SCALE = math.log2(math.e) / math.sqrt(HEAD_DIM)
VMEM_LIMIT = 56 << 20

bf16 = jnp.bfloat16
f32 = jnp.float32
NT = (((1,), (1,)), ((), ()))


def resident(shape):
    return pl.BlockSpec(shape, lambda *_: (0,) * len(shape), pipeline_mode=pl.Buffered(1))


def head_lanes(head):
    first, last = HEAD_DIM * head, HEAD_DIM * (head + 1) - 1
    return first // 128 * 128, (last // 128 + 1) * 128


def encode_kernel(
    half_ref, own_ref, other_ref, gain_ref, bias_ref, wqkv_ref, wout_ref, place_ref, out_ref,
    x_s, normed_s, qk_s, vt_s, ctx_s,
):
    for s in range(2):
        x_s[s * PATCH : s * PATCH + HALF, :] = own_ref[s]
        x_s[s * PATCH + HALF : (s + 1) * PATCH, :] = other_ref[s]
    for r in range(0, 2 * PATCH, HALF):
        rows = x_s[r : r + HALF, :].astype(f32)
        centred = rows - jnp.sum(rows, -1, keepdims=True) * (1.0 / D)
        variance = jnp.sum(centred * centred, -1, keepdims=True) * (1.0 / D)
        normed = centred * lax.rsqrt(variance + NORM_EPS) * gain_ref[...] + bias_ref[...]
        normed_s[r : r + HALF, :] = normed.astype(bf16)
    for c in range(0, 2 * D, 256):
        part = jnp.dot(normed_s[...], wqkv_ref[:, c : c + 256], preferred_element_type=f32)
        qk_s[:, c : c + 256] = part.astype(bf16)
    for c in range(0, D, 128):
        first = 2 * D + c
        part = jnp.dot(normed_s[...], wqkv_ref[:, first : first + 128], preferred_element_type=f32)
        vt_s[c : c + 128, :] = part.T
    lane = lax.broadcasted_iota(jnp.int32, (1, D), 1)
    ones = jnp.ones((8, PATCH), f32)
    for s in range(2):
        rows = slice(s * PATCH, (s + 1) * PATCH)
        for head in range(HEADS):
            lo, hi = head_lanes(head)
            start = HEAD_DIM * head
            mine = (lane[:, lo:hi] >= start) & (lane[:, lo:hi] < start + HEAD_DIM)
            keys = qk_s[rows, D + lo : D + hi]
            keys = jnp.where(mine, keys, jnp.zeros_like(keys))
            scores = lax.dot_general(keys, qk_s[rows, lo:hi], NT, preferred_element_type=f32)
            top = jnp.max(scores, 0, keepdims=True)
            weights = jnp.exp2((scores - top) * SCORE_SCALE).astype(bf16)
            values = jnp.concatenate([vt_s[start : start + HEAD_DIM, rows], ones], 0).astype(bf16)
            summed = jnp.dot(values, weights, preferred_element_type=f32)
            ctx_s[start : start + HEAD_DIM, rows] = summed[:HEAD_DIM] / summed[HEAD_DIM : HEAD_DIM + 1]
    row = lax.broadcasted_iota(jnp.int32, (2 * BLOCKS, 2 * PATCH), 0)
    col = lax.broadcasted_iota(jnp.int32, (2 * BLOCKS, 2 * PATCH), 1)
    member = (row // 2 == place_ref[...]) & (row % 2 == col // PATCH)
    pool = jnp.where(member, 0.25, 0.0).astype(bf16)
    pooled_ctx = lax.dot_general(pool, ctx_s[...].astype(bf16), NT, preferred_element_type=f32)
    total = jnp.dot(pool, x_s[...], preferred_element_type=f32)
    total += jnp.dot(pooled_ctx.astype(bf16), wout_ref[...], preferred_element_type=f32)
    out_ref[...] = total.astype(bf16).reshape(BLOCKS, 2, D)


def encode(half, frames_in, other, gain, bias, w_qkv, w_out, place):
    return pl.pallas_call(
        encode_kernel,
        grid_spec=pltpu.PrefetchScalarGridSpec(
            num_scalar_prefetch=1,
            grid=(PAIRS,),
            in_specs=[
                pl.BlockSpec((2, HALF, D), lambda i, half: (half[0] * PAIRS + i, 0, 0)),
                pl.BlockSpec((2, HALF, D), lambda i, half: (i, 0, 0)),
                resident((1, D)),
                resident((1, D)),
                resident((D, 3 * D)),
                resident((D, D)),
                resident((1, 2 * PATCH)),
            ],
            out_specs=pl.BlockSpec((BLOCKS, 2, D), lambda i, half: (0, 0, i)),
            scratch_shapes=[
                pltpu.VMEM((2 * PATCH, D), bf16),
                pltpu.VMEM((2 * PATCH, D), bf16),
                pltpu.VMEM((2 * PATCH, 2 * D), bf16),
                pltpu.VMEM((D, 2 * PATCH), f32),
                pltpu.VMEM((D, 2 * PATCH), f32),
            ],
        ),
        out_shape=jax.ShapeDtypeStruct((BLOCKS, 2, PAIRS * D), bf16),
        compiler_params=pltpu.CompilerParams(vmem_limit_bytes=VMEM_LIMIT),
        name="encode_frames",
    )(half, frames_in, other, gain, bias, w_qkv, w_out, place)


def mix_kernel(lengths_ref, held_ref, own_ref, other_ref, taps_ref, out_ref, rows_s):
    step = pl.program_id(0)

    @pl.when(step == 0)
    def _():
        for j in range(PAIRS):
            cols = slice(j * D, (j + 1) * D)
            rows_s[j * 128 : (j + 1) * 128, :] = own_ref[:, :, cols].reshape(128, D)
            rows_s[(j + 3) * 128 : (j + 4) * 128, :] = other_ref[:, :, cols].reshape(128, D)

    row = lax.broadcasted_iota(jnp.int32, (128, 1), 0)
    frame = FR_DEV * (row // 2) + 2 * step + row % 2
    first, last = frame < 0, frame + 1 == FRAMES
    start = 0
    for c in range(CLIPS):
        first |= frame == start
        last |= frame + 1 == start
        start += lengths_ref[c]
    held = held_ref[...]

    def pick(wanted):
        hit = jnp.where(held == wanted, 1.0, 0.0).astype(bf16)
        return jnp.dot(hit, rows_s[...], preferred_element_type=f32)

    earlier = pick(jnp.where(first, -2, frame - 1))
    later = pick(jnp.where(last, -2, frame + 1))
    mixed = taps_ref[0:1] * earlier + taps_ref[1:2] * pick(frame) + taps_ref[2:3] * later
    out_ref[...] = mixed.astype(bf16).reshape(FRAME_DEVS, 2, D)


def mix(lengths, held, own, other, taps):
    return pl.pallas_call(
        mix_kernel,
        grid=(PAIRS,),
        in_specs=[
            pl.BlockSpec(memory_space=pltpu.SMEM),
            resident((1, 768)),
            resident((FRAME_DEVS, 2, PAIRS * D)),
            resident((FRAME_DEVS, 2, PAIRS * D)),
            resident((3, D)),
        ],
        out_specs=pl.BlockSpec((FRAME_DEVS, 2, D), lambda i: (0, 0, i)),
        out_shape=jax.ShapeDtypeStruct((FRAME_DEVS, 2, PAIRS * D), bf16),
        scratch_shapes=[pltpu.VMEM((768, D), bf16)],
        compiler_params=pltpu.CompilerParams(vmem_limit_bytes=VMEM_LIMIT),
        name="mix_rows",
    )(lengths, held, own, other, taps)


def project_kernel(mixed_ref, w_ref, out_ref):
    row = lax.broadcasted_iota(jnp.int32, (128, 128), 0)
    col = lax.broadcasted_iota(jnp.int32, (128, 128), 1)
    swap = jnp.where(col == 2 * (row % BLOCKS) + row // BLOCKS, 1.0, 0.0).astype(bf16)
    rows = mixed_ref[...].reshape(128, D)
    rows = jnp.dot(swap, rows, preferred_element_type=f32).astype(bf16)
    out = jnp.dot(rows, w_ref[...], preferred_element_type=f32).astype(bf16)
    out_ref[...] = out.reshape(2, BLOCKS, OUT_DEV)


def project(mixed, w_proj):
    return pl.pallas_call(
        project_kernel,
        grid=(PAIRS,),
        in_specs=[
            pl.BlockSpec((BLOCKS, 2, D), lambda i: (0, 0, i)),
            resident((D, OUT_DEV)),
        ],
        out_specs=pl.BlockSpec((2, BLOCKS, OUT_DEV), lambda i: (i, 0, 0)),
        out_shape=jax.ShapeDtypeStruct((FR_DEV, BLOCKS, OUT_DEV), bf16),
        compiler_params=pltpu.CompilerParams(vmem_limit_bytes=VMEM_LIMIT),
        name="project_rows",
    )(mixed, w_proj)


SWAP = [(0, 1), (1, 0)]


def on_device(
    frames_in, norm_gain, norm_bias, w_qkv, w_out, time_taps, w_proj, clip_lengths, frame_slot, block_map
):
    tile = lax.axis_index("tile")
    sent = lax.dynamic_slice_in_dim(frames_in, FR_DEV * (1 - tile), FR_DEV)
    other = lax.ppermute(sent, "tile", SWAP)
    halves = block_map.reshape(2, BLOCKS // 2)
    place = jnp.where(tile == 0, halves, halves[::-1]).reshape(BLOCKS)
    place = jnp.tile(jnp.repeat(place, 4), 2)[None]
    half = jnp.reshape(tile, (1,)).astype(jnp.int32)
    pooled = encode(
        half, frames_in, other, norm_gain[None], norm_bias[None], w_qkv, w_out, place
    )
    spread = lax.all_to_all(pooled, "frame", split_axis=0, concat_axis=0, tiled=True)
    spread_other = lax.ppermute(spread, "tile", SWAP)
    held = frame_slot.reshape(FRAME_DEVS, 2, PAIRS, 2).transpose(1, 2, 0, 3)
    held = jnp.where(tile == 0, held, held[::-1]).reshape(1, 768)
    mixed = mix(clip_lengths, held, spread, spread_other, time_taps)
    home = lax.all_to_all(mixed, "frame", split_axis=0, concat_axis=0, tiled=True)
    return project(home, w_proj)


def solution(mesh):
    in_specs = (P("frame", "tile", None), P(), P(), P(), P(), P(), P(None, "tile"), P(), P(), P())
    return jax.shard_map(
        on_device, mesh=mesh, in_specs=in_specs, out_specs=P("frame", None, "tile"), check_vma=False
    )
```

profile of v0, /device:TPU:1, one launch (start us, length us, event | category | flops | bytes accessed | tf_op | source)
XLA Modules:
  0.0 125.7 jit_solution(10198626048466316079)
XLA Ops:
  0.0 0.0 copy-start.3
  0.0 0.0 copy-start.4
  0.0 1.6 %constant_dynamic-slice_fusion = bf16[6,128,1152]{2,1,0:T(8,128)(2,1)S(1)} fusion(bf16[12,128,1152]{2,1,0:T(8,128)(2,1)} %own_ref.1, s32[]{:T(128)S(6)} %select_n.21), kind=kLoop, calls=%fused_computation.3 | loop fusion | bytes 3538948 | tf_op jit(solution)/shard_map/dynamic_slice | solution.py:198
  1.7 1.5 %collective-permute-start = (bf16[6,128,1152]{2,1,0:T(8,128)(2,1)S(1)}, bf16[6,128,1152]{2,1,0:T(8,128)(2,1)S(1)}, u32[]{:S(2)}, u32[]{:S(2)}) collective-permute-start(bf16[6,128,1152]{2,1,0:T(8,128)(2,1)S(1)} %constant_dynamic-slice_fusion), channel_id=1, source_target_pairs={{0,1},{1,0},{2,3},{3,2},{4,5},{5,4},{6,7},{7,6},{8,9},{9,8},{10,11... | collective-permute-start | bytes 5308424 | tf_op jit(solution)/shard_map/ppermute | solution.py:199
  3.2 1.3 %reshape.19 = s32[2,32]{1,0:T(2,128)} reshape(s32[64]{0:T(128)} %param.19) | data formatting | bytes 512 | tf_op jit(solution)/shard_map/reshape | solution.py:200
  4.5 1.3 %rev.7 = s32[2,32]{1,0:T(2,128)} reverse(s32[2,32]{1,0:T(2,128)} %reshape.19), dimensions={0} | reverse | bytes 512 | tf_op jit(solution)/shard_map/rev | solution.py:201
  5.7 1.2 broadcast_select_fusion
  6.9 1.3 %reshape.20 = s32[64]{0:T(128)} reshape(s32[2,32]{1,0:T(2,128)} %broadcast_select_fusion) | data formatting | bytes 512 | tf_op jit(solution)/shard_map/reshape | solution.py:201
  8.2 1.3 %broadcast_in_dim.11 = s32[64,4]{1,0:T(8,128)} broadcast(s32[64]{0:T(128)} %reshape.20), dimensions={0} | broadcast | bytes 1280 | tf_op jit(solution)/shard_map/broadcast_in_dim | solution.py:202
  9.5 1.4 %tile.7 = s32[256]{0:T(256)} reshape(s32[64,4]{1,0:T(8,128)} %broadcast_in_dim.11) | data formatting | bytes 2048 | tf_op jit(solution)/shard_map/tile | solution.py:202
  10.9 0.7 broadcast_bitcast_fusion
  11.6 0.6 copy.12
  12.2 0.0 copy-done.3
  12.2 0.6 broadcast_in_dim.10.bias_ref
  12.8 0.0 copy-done.4
  12.8 0.6 broadcast_in_dim.9.gain_ref
  13.4 0.0 collective-permute-done.other_ref
  13.4 0.0 copy-start.1
  13.4 1.2 copy-done.1
  14.6 0.0 copy-start.5
  14.6 45.2 %encode_frames.1 = bf16[64,2,3456]{2,1,0:T(2,128)(2,1)} custom-call(s32[1]{0:T(128)} %bitcast.1.half_ref, bf16[12,128,1152]{2,1,0:T(8,128)(2,1)} %own_ref.1, bf16[6,128,1152]{2,1,0:T(8,128)(2,1)} %copy-done.1, f32[1,1152]{1,0:T(1,128)} %broadcast_in_dim.9.gain_ref, f32[1,1152]{1,0:T(1,128)} %broadcast_in_dim.10.bias_ref, bf16[1152,3456]{1,0:T(8,128)(2,1)} %wqkv_ref.1, ...), custom_call_target="tpu_custom_call" | custom-call | tf_op jit(solution)/shard_map/encode_frames/pallas_call | solution.py:88
  59.8 27.8 %all_to_all.10.own_ref = bf16[64,2,3456]{2,1,0:T(2,128)(2,1)S(1)} all-to-all(bf16[64,2,3456]{2,1,0:T(2,128)(2,1)} %encode_frames.1), channel_id=1, replica_groups=mesh['frame'=64,'tile'=2] {'frame'}, dimensions={0} | all-to-all | bytes 1769472 | tf_op jit(solution)/shard_map/all_to_all | solution.py:207
  87.6 1.6 %collective-permute-start.1 = (bf16[64,2,3456]{2,1,0:T(2,128)(2,1)S(1)}, bf16[64,2,3456]{2,1,0:T(2,128)(2,1)S(1)}, u32[]{:S(2)}, u32[]{:S(2)}) collective-permute-start(bf16[64,2,3456]{2,1,0:T(2,128)(2,1)S(1)} %all_to_all.10.own_ref), channel_id=1, source_target_pairs={{0,1},{1,0},{2,3},{3,2},{4,5},{5,4},{6,7},{7,6},{8,9},{9,8},{10,11... | collective-permute-start | bytes 2654216 | tf_op jit(solution)/shard_map/ppermute | solution.py:208
  89.2 0.0 copy-done.5
  89.2 0.2 reshape.16
  89.5 0.8 reshape.17.held_ref
  90.2 1.0 collective-permute-done.1.other_ref
  91.2 0.0 copy-done
  91.2 0.9 copy-done.2
  92.2 5.5 %mix_rows.1 = bf16[64,2,3456]{2,1,0:T(2,128)(2,1)} custom-call(s32[6]{0:T(128)} %lengths_ref.1, s32[1,768]{1,0:T(1,128)} %reshape.17.held_ref, bf16[64,2,3456]{2,1,0:T(2,128)(2,1)} %copy-done, bf16[64,2,3456]{2,1,0:T(2,128)(2,1)} %copy-done.2, f32[3,1152]{1,0:T(4,128)} %taps_ref.1), custom_call_target="tpu_custom_call" | custom-call | tf_op jit(solution)/shard_map/mix_rows/pallas_call | solution.py:148
  97.6 22.0 %all_to_all.11.mixed_ref = bf16[64,2,3456]{2,1,0:T(2,128)(2,1)} all-to-all(bf16[64,2,3456]{2,1,0:T(2,128)(2,1)} %mix_rows.1), channel_id=1, replica_groups=mesh['frame'=64,'tile'=2] {'frame'}, dimensions={0} | all-to-all | bytes 1769472 | tf_op jit(solution)/shard_map/all_to_all | solution.py:212
  119.6 6.1 %project_rows.1 = bf16[6,64,1792]{2,1,0:T(8,128)(2,1)} custom-call(bf16[64,2,3456]{2,1,0:T(2,128)(2,1)} %all_to_all.11.mixed_ref, bf16[1152,1792]{1,0:T(8,128)(2,1)} %w_ref.1), custom_call_target="tpu_custom_call" | custom-call | tf_op jit(solution)/shard_map/project_rows/pallas_call | solution.py:177
  (4 shorter events, 0.1 us)
Async XLA Ops:
  0.0 12.2 %copy-start.3 = (f32[1152]{0:T(1024)S(1)}, f32[1152]{0:T(1024)}, u32[]{:S(2)}) copy-start(f32[1152]{0:T(1024)} %param.12) | copy-start | bytes 13828
  0.0 12.8 %copy-start.4 = (f32[1152]{0:T(1024)S(1)}, f32[1152]{0:T(1024)}, u32[]{:S(2)}) copy-start(f32[1152]{0:T(1024)} %param.11) | copy-start | bytes 13828
  1.7 11.7 %collective-permute-start = (bf16[6,128,1152]{2,1,0:T(8,128)(2,1)S(1)}, bf16[6,128,1152]{2,1,0:T(8,128)(2,1)S(1)}, u32[]{:S(2)}, u32[]{:S(2)}) collective-permute-start(bf16[6,128,1152]{2,1,0:T(8,128)(2,1)S(1)} %constant_dynamic-slice_fusion), channel_id=1, source_target_pairs={{0,1},{1,0},{2,3},{3,2},{4,5},{5,4},{6,7},{7,6},{8,9},{9,8},{10,11... | collective-permute-start | bytes 5308424 | tf_op jit(solution)/shard_map/ppermute | solution.py:199
  13.4 1.2 copy-start.1
  14.6 74.6 %copy-start.5 = (s32[768]{0:T(1024)S(1)}, s32[768]{0:T(1024)}, u32[]{:S(2)}) copy-start(s32[768]{0:T(1024)} %param.18) | copy-start | bytes 9220
  87.6 3.6 %copy-start = (bf16[64,2,3456]{2,1,0:T(2,128)(2,1)}, bf16[64,2,3456]{2,1,0:T(2,128)(2,1)S(1)}, u32[]{:S(2)}) copy-start(bf16[64,2,3456]{2,1,0:T(2,128)(2,1)S(1)} %all_to_all.10.own_ref) | copy-start | bytes 2654212
  87.6 3.6 %collective-permute-start.1 = (bf16[64,2,3456]{2,1,0:T(2,128)(2,1)S(1)}, bf16[64,2,3456]{2,1,0:T(2,128)(2,1)S(1)}, u32[]{:S(2)}, u32[]{:S(2)}) collective-permute-start(bf16[64,2,3456]{2,1,0:T(2,128)(2,1)S(1)} %all_to_all.10.own_ref), channel_id=1, source_target_pairs={{0,1},{1,0},{2,3},{3,2},{4,5},{5,4},{6,7},{7,6},{8,9},{9,8},{10,11... | collective-permute-start | bytes 2654216 | tf_op jit(solution)/shard_map/ppermute | solution.py:208
  91.2 0.9 copy-start.2
where the time goes:
time: 126 us
  Pallas kernels  56.8 us (45%)
  blocking collectives  49.7 us (39%)
  local copies, waits for them, and re-layouts  13.8 us (11%)
  starting transfers between devices  3.05 us (2%)
  other arithmetic  1.27 us (1%)
    pallas_call x1, Pallas kernels, encode(): pl.pallas_call(encode_kernel, grid_spec=pltpu.PrefetchScalarGridSpec(num_...  45.2 us
    all_to_all x1, blocking collectives, on_device(): lax.all_to_all(pooled, 'frame', split_axis=0, concat_axis=0, tiled=True)  27.8 us
    all_to_all x1, blocking collectives, on_device(): lax.all_to_all(mixed, 'frame', split_axis=0, concat_axis=0, tiled=True)  22 us
    pallas_call x1, Pallas kernels, project(): pl.pallas_call(project_kernel, grid=(PAIRS,), in_specs=[pl.BlockSpec((BLO...  6.09 us
    pallas_call x1, Pallas kernels, mix(): pl.pallas_call(mix_kernel, grid=(PAIRS,), in_specs=[pl.BlockSpec(memory_s...  5.46 us
    unnamed x14, local copies, waits for them, and re-layouts  3.43 us
  transfers between devices with their start and end apart: 2, of which 1 were waited for; matrix products, arithmetic and copies ran while one was open for 9% of the time, Pallas kernels for 0%

commit v1 on v0

v1 whole, which is shorter than its diff:
```python
import math

import jax
import jax.numpy as jnp
from jax import lax
from jax.experimental import pallas as pl
from jax.experimental.pallas import tpu as pltpu
from jax.sharding import PartitionSpec as P

D = 1152
HEADS = 16
HEAD_DIM = 72
PATCH = 256
HALF = 128
BLOCKS = 64
FRAMES = 384
FRAME_DEVS = 64
CLIPS = 6
FR_DEV = 6
SLOT_DEV = 12
SLOTS = 768
PAIRS = 3
OUT_DEV = 1792
NORM_EPS = 1e-6
SCORE_SCALE = math.log2(math.e) / math.sqrt(HEAD_DIM)
ENCODE_VMEM = 34 << 20
SMALL_VMEM = 20 << 20

bf16 = jnp.bfloat16
f32 = jnp.float32
NT = (((1,), (1,)), ((), ()))


def resident(shape):
    return pl.BlockSpec(shape, lambda *_: (0,) * len(shape), pipeline_mode=pl.Buffered(1))


def anywhere():
    return pl.BlockSpec(memory_space=pl.ANY)


def head_lanes(head):
    first, last = HEAD_DIM * head, HEAD_DIM * (head + 1) - 1
    return first // 128 * 128, (last // 128 + 1) * 128


def in_vmem(x):
    return pltpu.with_memory_space_constraint(x, pltpu.VMEM)


def normalise(pieces, gain_ref, bias_ref, normed_s):
    gain, bias = gain_ref[...].reshape(1, D), bias_ref[...].reshape(1, D)
    for n, piece in enumerate(pieces):
        rows = piece[...].astype(f32)
        centred = rows - jnp.sum(rows, -1, keepdims=True) * (1.0 / D)
        variance = jnp.sum(centred * centred, -1, keepdims=True) * (1.0 / D)
        normed = centred * lax.rsqrt(variance + NORM_EPS) * gain + bias
        normed_s[n * HALF : (n + 1) * HALF, :] = normed.astype(bf16)


def project_qkv(normed_s, w_ref, qk_s, vt_s):
    for lo in range(0, 3 * D, 256):
        hi = min(lo + 256, 3 * D)
        part = jnp.dot(normed_s[...], w_ref[:, lo:hi], preferred_element_type=f32)
        if hi <= 2 * D:
            qk_s[:, lo:hi] = part.astype(bf16)
        else:
            vt_s[lo - 2 * D : hi - 2 * D, :] = part.T.astype(bf16)


def attend(qk_s, vt_s, ctx_s):
    lane = lax.broadcasted_iota(jnp.int32, (1, D), 1)
    ones = jnp.ones((16, PATCH), bf16)

    def scores(s, head):
        lo, hi = head_lanes(head)
        start = HEAD_DIM * head
        mine = (lane[:, lo:hi] >= start) & (lane[:, lo:hi] < start + HEAD_DIM)
        rows = slice(s * PATCH, (s + 1) * PATCH)
        keys = qk_s[rows, D + lo : D + hi]
        keys = jnp.where(mine, keys, jnp.zeros_like(keys))
        return lax.dot_general(keys, qk_s[rows, lo:hi], NT, preferred_element_type=f32)

    def weigh(score):
        top = jnp.max(score, 0, keepdims=True)
        return jnp.exp2((score - top) * SCORE_SCALE).astype(bf16)

    def total(s, head, weights):
        skip = 8 * (head % 2)
        first = HEAD_DIM * head - skip
        cols = slice(s * PATCH, (s + 1) * PATCH)
        values = jnp.concatenate([vt_s[first : first + 80, cols], ones], 0)
        summed = jnp.dot(values, weights, preferred_element_type=f32)
        ctx_s[HEAD_DIM * head : HEAD_DIM * (head + 1), cols] = (
            summed[skip : skip + HEAD_DIM] / summed[80:81]
        )

    items = [(s, head) for s in range(2) for head in range(HEADS)]
    score, weights = {}, {}
    for n in range(-4, len(items)):
        if n + 4 < len(items):
            score[n + 4] = scores(*items[n + 4])
        if 0 <= n + 2 < len(items):
            weights[n + 2] = weigh(score.pop(n + 2))
        if n >= 0:
            total(*items[n], weights.pop(n))


def pooling(tile, map_ref):
    block = lax.broadcasted_iota(jnp.int32, (BLOCKS, 2 * PATCH), 0)
    col = lax.broadcasted_iota(jnp.int32, (BLOCKS, 2 * PATCH), 1)
    col_block = (col % HALF) // 4 + BLOCKS // 2 * ((col // HALF + tile) % 2)
    row = lax.broadcasted_iota(jnp.int32, (2 * BLOCKS, 1), 0)
    placing = jnp.where(map_ref[...] == row // 2, 1.0, 0.0).astype(bf16)
    member = jnp.where(block == col_block, 0.25, 0.0).astype(bf16)
    member = jnp.dot(placing, member, preferred_element_type=f32)
    frame_of = lax.broadcasted_iota(jnp.int32, (1, 2 * PATCH), 1) // PATCH
    return jnp.where(frame_of == row % 2, member, 0.0).astype(bf16)


def encode_kernel(
    tile_ref, own_ref, other_ref, gain_ref, bias_ref, wqkv_ref, wout_ref, map_ref, out_ref,
    normed_s, qk_s, vt_s, ctx_s, pooled_x, pooled_ctx, pool_s,
):
    pool_s[...] = pooling(tile_ref[0], map_ref)

    def one_pair(pair, carry):
        pieces = [ref.at[2 * pair + s] for s in range(2) for ref in (own_ref, other_ref)]
        normalise(pieces, gain_ref, bias_ref, normed_s)
        project_qkv(normed_s, wqkv_ref, qk_s, vt_s)
        attend(qk_s, vt_s, ctx_s)
        rows = pl.ds(pl.multiple_of(pair * 2 * BLOCKS, 2 * BLOCKS), 2 * BLOCKS)
        pooled = lax.dot_general(
            pool_s[...], ctx_s[...].astype(bf16), NT, preferred_element_type=f32
        )
        pooled_ctx[rows, :] = pooled.astype(bf16)
        patches = jnp.concatenate([piece[...] for piece in pieces], 0)
        pooled_x[rows, :] = jnp.dot(pool_s[...], patches, preferred_element_type=f32)
        return carry

    lax.fori_loop(0, PAIRS, one_pair, 0)
    for pair in range(PAIRS):
        rows = slice(pair * 2 * BLOCKS, (pair + 1) * 2 * BLOCKS)
        total = jnp.dot(pooled_ctx[rows, :], wout_ref[...], preferred_element_type=f32)
        total = (total + pooled_x[rows, :]).astype(bf16)
        out_ref[:, :, pair * D : (pair + 1) * D] = total.reshape(BLOCKS, 2, D)


def encode(tile, own, other, gain, bias, w_qkv, w_out, block_map):
    vmem = pl.BlockSpec(memory_space=pltpu.VMEM)
    return pl.pallas_call(
        encode_kernel,
        in_specs=[pl.BlockSpec(memory_space=pltpu.SMEM)] + [vmem] * 7,
        out_specs=vmem,
        out_shape=jax.ShapeDtypeStruct((BLOCKS, 2, PAIRS * D), bf16),
        scratch_shapes=[
            pltpu.VMEM((2 * PATCH, D), bf16),
            pltpu.VMEM((2 * PATCH, 2 * D), bf16),
            pltpu.VMEM((D, 2 * PATCH), bf16),
            pltpu.VMEM((D, 2 * PATCH), f32),
            pltpu.VMEM((PAIRS * 2 * BLOCKS, D), f32),
            pltpu.VMEM((PAIRS * 2 * BLOCKS, D), bf16),
            pltpu.VMEM((2 * BLOCKS, 2 * PATCH), bf16),
        ],
        compiler_params=pltpu.CompilerParams(vmem_limit_bytes=ENCODE_VMEM),
        name="encode_frames",
    )(tile, in_vmem(own), in_vmem(other), gain, bias, in_vmem(w_qkv), in_vmem(w_out), block_map)


def mix_kernel(tile_ref, lengths_ref, slots_ref, own_ref, other_ref, taps_ref, out_ref, rows_s, held_s):
    step = pl.program_id(0)

    @pl.when(step == 0)
    def _():
        for j in range(PAIRS):
            cols = slice(j * D, (j + 1) * D)
            rows_s[j * 128 : (j + 1) * 128, :] = own_ref[:, :, cols].reshape(128, D)
            rows_s[(j + 3) * 128 : (j + 4) * 128, :] = other_ref[:, :, cols].reshape(128, D)
        code = slots_ref[...] + 1
        code = jnp.concatenate([code // 16, code % 16] + [jnp.zeros_like(code)] * 6, 0)
        slot = lax.broadcasted_iota(jnp.int32, (SLOTS, SLOTS), 0)
        col = lax.broadcasted_iota(jnp.int32, (1, SLOTS), 1)
        group, place = col // 128, col % 128
        core = (group // PAIRS + tile_ref[0]) % 2
        source = SLOT_DEV * (place // 2) + FR_DEV * core + 2 * (group % PAIRS) + place % 2
        moved = jnp.where(slot == source, 1.0, 0.0).astype(bf16)
        code = jnp.dot(code.astype(f32).astype(bf16), moved, preferred_element_type=f32)
        held_s[...] = (code[0:1] * 16.0 + code[1:2]).astype(jnp.int32) - 1

    row = lax.broadcasted_iota(jnp.int32, (128, 1), 0)
    frame = FR_DEV * (row // 2) + 2 * step + row % 2
    first, last = frame < 0, frame + 1 == FRAMES
    start = 0
    for c in range(CLIPS):
        first |= frame == start
        last |= frame + 1 == start
        start += lengths_ref[c]
    held = held_s[...]

    def pick(wanted):
        hit = jnp.where(held == wanted, 1.0, 0.0).astype(bf16)
        return jnp.dot(hit, rows_s[...], preferred_element_type=f32)

    earlier = pick(jnp.where(first, -2, frame - 1))
    later = pick(jnp.where(last, -2, frame + 1))
    mixed = taps_ref[0:1] * earlier + taps_ref[1:2] * pick(frame) + taps_ref[2:3] * later
    out_ref[...] = mixed.astype(bf16).reshape(FRAME_DEVS, 2, D)


def mix(tile, lengths, slots, own, other, taps):
    return pl.pallas_call(
        mix_kernel,
        grid=(PAIRS,),
        in_specs=[
            pl.BlockSpec(memory_space=pltpu.SMEM),
            pl.BlockSpec(memory_space=pltpu.SMEM),
            resident((1, SLOTS)),
            resident((FRAME_DEVS, 2, PAIRS * D)),
            resident((FRAME_DEVS, 2, PAIRS * D)),
            resident((3, D)),
        ],
        out_specs=pl.BlockSpec((FRAME_DEVS, 2, D), lambda i: (0, 0, i)),
        out_shape=jax.ShapeDtypeStruct((FRAME_DEVS, 2, PAIRS * D), bf16),
        scratch_shapes=[pltpu.VMEM((SLOTS, D), bf16), pltpu.VMEM((1, SLOTS), jnp.int32)],
        compiler_params=pltpu.CompilerParams(vmem_limit_bytes=SMALL_VMEM),
        name="mix_rows",
    )(tile, lengths, slots, own, other, taps)


def project_kernel(mixed_ref, w_ref, out_ref):
    row = lax.broadcasted_iota(jnp.int32, (128, 128), 0)
    col = lax.broadcasted_iota(jnp.int32, (128, 128), 1)
    swap = jnp.where(col == 2 * (row % BLOCKS) + row // BLOCKS, 1.0, 0.0).astype(bf16)
    rows = mixed_ref[...].reshape(128, D)
    rows = jnp.dot(swap, rows, preferred_element_type=f32).astype(bf16)
    out = jnp.dot(rows, w_ref[...], preferred_element_type=f32).astype(bf16)
    out_ref[...] = out.reshape(2, BLOCKS, OUT_DEV)


def project(mixed, w_proj):
    return pl.pallas_call(
        project_kernel,
        grid=(PAIRS,),
        in_specs=[
            pl.BlockSpec((BLOCKS, 2, D), lambda i: (0, 0, i)),
            resident((D, OUT_DEV)),
        ],
        out_specs=pl.BlockSpec((2, BLOCKS, OUT_DEV), lambda i: (i, 0, 0)),
        out_shape=jax.ShapeDtypeStruct((FR_DEV, BLOCKS, OUT_DEV), bf16),
        compiler_params=pltpu.CompilerParams(vmem_limit_bytes=SMALL_VMEM),
        name="project_rows",
    )(mixed, w_proj)


SWAP = [(0, 1), (1, 0)]


def on_device(
    frames_in, norm_gain, norm_bias, w_qkv, w_out, time_taps, w_proj, clip_lengths, frame_slot, block_map
):
    tile = lax.axis_index("tile")
    sent = lax.dynamic_slice_in_dim(frames_in, FR_DEV * (1 - tile), FR_DEV)
    other = lax.ppermute(sent, "tile", SWAP)
    core = jnp.reshape(tile, (1,)).astype(jnp.int32)
    own = lax.dynamic_slice_in_dim(frames_in, FR_DEV * tile, FR_DEV)
    pooled = encode(
        core, own, other, norm_gain, norm_bias, w_qkv, w_out, block_map[None]
    )
    spread = lax.all_to_all(pooled, "frame", split_axis=0, concat_axis=0, tiled=True)
    spread_other = lax.ppermute(spread, "tile", SWAP)
    mixed = mix(core, clip_lengths, frame_slot[None], spread, spread_other, time_taps)
    home = lax.all_to_all(mixed, "frame", split_axis=0, concat_axis=0, tiled=True)
    return project(home, w_proj)


def solution(mesh):
    in_specs = (P("frame", "tile", None), P(), P(), P(), P(), P(), P(None, "tile"), P(), P(), P())
    return jax.shard_map(
        on_device, mesh=mesh, in_specs=in_specs, out_specs=P("frame", None, "tile"), check_vma=False
    )
```

time: 126 us -> 98.7 us (0.78)
  Pallas kernels: 56.8 us -> 35.6 us
  local copies, waits for them, and re-layouts: 13.8 us -> 5.74 us
  waiting for transfers between devices: 1 us -> 5.36 us
  blocking collectives: 49.7 us -> 47.9 us
  other arithmetic: 1.27 us -> 0 us
    pallas_call x1, Pallas kernels: 45.2 us -> 27.5 us  [encode(): pl.pallas_call(encode_kernel, in_specs=[pl.BlockSpec(memory_space=pltpu.S...]
    reshape x4 -> x0, local copies, waits for them, and re-layouts: 3.5 us -> none  [the longest x1 1.3 us: on_device(): halves = block_map.reshape(2, BLOCKS // 2)]
    ppermute x1, waiting for transfers between devices: 0.01 us -> 3.32 us  [on_device(): other = lax.ppermute(sent, 'tile', SWAP)]
    broadcast_in_dim x3 -> x1, local copies, waits for them, and re-layouts: 2.48 us -> 0.01 us  [on_device(): frame_slot[None]]
    pallas_call x1, Pallas kernels: 6.09 us -> 3.8 us  [project(): pl.pallas_call(project_kernel, grid=(PAIRS,), in_specs=[pl.BlockSpec((BLO...]
    all_to_all x1, blocking collectives: 22 us -> 20.4 us  [on_device(): lax.all_to_all(mixed, 'frame', split_axis=0, concat_axis=0, tiled=True)]
    another operation x1 -> x0, local copies, waits for them, and re-layouts: 1.44 us -> none  [on_device(): place = jnp.tile(jnp.repeat(place, 4), 2)[None]]
    select_n x2 -> x0, other arithmetic: 1.27 us -> none  [the longest x1 1.23 us: on_device(): place = jnp.where(tile == 0, halves, halves[::-1]).reshape(BLOCKS)]
  transfers between devices with their start and end apart: 2 -> 2, of which waited for: 1 -> 2; matrix products, arithmetic and copies ran while one was open for 9% -> 0% of each run, Pallas kernels for 0% -> 0%
where the time goes in v1:
time: 98.7 us; the launch traced here: 98 us
  blocking collectives  47.9 us (49%)
  Pallas kernels  35.6 us (36%)
  local copies, waits for them, and re-layouts  5.74 us (6%)
  waiting for transfers between devices  5.36 us (5%)
  starting transfers between devices  3.35 us (3%)
    pallas_call x1, Pallas kernels, encode(): pl.pallas_call(encode_kernel, in_specs=[pl.BlockSpec(memory_space=pltpu.S...  27.5 us
    all_to_all x1, blocking collectives, on_device(): lax.all_to_all(pooled, 'frame', split_axis=0, concat_axis=0, tiled=True)  27.4 us
    all_to_all x1, blocking collectives, on_device(): lax.all_to_all(mixed, 'frame', split_axis=0, concat_axis=0, tiled=True)  20.4 us
    pallas_call x1, Pallas kernels, mix(): pl.pallas_call(mix_kernel, grid=(PAIRS,), in_specs=[pl.BlockSpec(memory_s...  4.29 us
    pallas_call x1, Pallas kernels, project(): pl.pallas_call(project_kernel, grid=(PAIRS,), in_specs=[pl.BlockSpec((BLO...  3.8 us
    ppermute x1, waiting for transfers between devices, on_device(): other = lax.ppermute(sent, 'tile', SWAP)  3.32 us
    unnamed x18, local copies, waits for them, and re-layouts  3.29 us
    dynamic_slice x1, local copies, waits for them, and re-layouts, on_device(): sent = lax.dynamic_slice_in_dim(frames_in, FR_DEV * (1 - tile), FR_DEV)  2.44 us
  transfers between devices with their start and end apart: 2, of which 2 were waited for; matrix products, arithmetic and copies ran while one was open for 0% of the time, Pallas kernels for 0%

profile of v1, /device:TPU:1, one launch (start us, length us, event | category | flops | bytes accessed | tf_op | source)
XLA Modules:
  0.0 98.0 jit_solution(3091766935140866981)
XLA Ops:
  0.0 0.0 copy-start.2
  0.0 0.0 copy-start.4
  0.0 0.0 copy-start.5
  0.0 0.0 copy-start.6
  0.0 2.4 %constant_dynamic-slice_fusion = (bf16[6,128,1152]{2,1,0:T(8,128)(2,1)S(1)}, bf16[6,128,1152]{2,1,0:T(8,128)(2,1)S(1)}) fusion(bf16[12,128,1152]{2,1,0:T(8,128)(2,1)} %param.10, s32[]{:T(128)S(6)} %select_n.7, s32[]{:T(128)S(6)} %select_n.6), kind=kLoop, calls=%fused_computation | loop fusion | bytes 7077896 | tf_op jit(solution)/shard_map/dynamic_slice | solution.py:262
  2.5 1.5 %collective-permute-start = (bf16[6,128,1152]{2,1,0:T(8,128)(2,1)S(1)}, bf16[6,128,1152]{2,1,0:T(8,128)(2,1)S(1)}, u32[]{:S(2)}, u32[]{:S(2)}) collective-permute-start(bf16[6,128,1152]{2,1,0:T(8,128)(2,1)S(1)} %get-tuple-element.5), channel_id=1, source_target_pairs={{0,1},{1,0},{2,3},{3,2},{4,5},{5,4},{6,7},{7,6},{8,9},{9,8},{10,11... | collective-permute-start | bytes 5308424 | tf_op jit(solution)/shard_map/ppermute | solution.py:263
  4.0 3.3 %collective-permute-done.other_ref = bf16[6,128,1152]{2,1,0:T(8,128)(2,1)S(1)} collective-permute-done((bf16[6,128,1152]{2,1,0:T(8,128)(2,1)S(1)}, bf16[6,128,1152]{2,1,0:T(8,128)(2,1)S(1)}, u32[]{:S(2)}, u32[]{:S(2)}) %collective-permute-start) | collective-permute-done | bytes 1769504 | tf_op jit(solution)/shard_map/ppermute | solution.py:263
  7.3 0.0 copy-done.2
  7.3 0.0 copy-done.4
  7.3 0.0 copy-done.5
  7.3 0.0 copy-done.6
  7.3 0.0 copy-start
  7.3 3.3 %copy-done = bf16[1152,3456]{1,0:T(8,128)(2,1)S(1)} copy-done((bf16[1152,3456]{1,0:T(8,128)(2,1)S(1)}, bf16[1152,3456]{1,0:T(8,128)(2,1)}, u32[]{:S(2)}) %copy-start) | copy-done | bytes 7962648
  10.6 27.5 %encode_frames.1 = bf16[64,2,3456]{2,1,0:T(2,128)(2,1)S(1)} custom-call(s32[1]{0:T(128)} %bitcast.tile_ref, bf16[6,128,1152]{2,1,0:T(8,128)(2,1)S(1)} %get-tuple-element.6.own_ref, bf16[6,128,1152]{2,1,0:T(8,128)(2,1)S(1)} %collective-permute-done.other_ref, f32[1152]{0:T(1024)S(1)} %copy-done.4, f32[1152]{0:T(1024)S(1)} %copy-done.5, ...), custom_call_target="tpu_custom_call" | custom-call | tf_op jit(solution)/shard_map/encode_frames/pallas_call | solution.py:151
  38.1 0.0 copy-start.8
  38.1 0.0 copy-start.3
  38.1 0.0 copy-start.7
  38.1 27.4 %all_to_all.10.own_ref = bf16[64,2,3456]{2,1,0:T(2,128)(2,1)S(1)} all-to-all(bf16[64,2,3456]{2,1,0:T(2,128)(2,1)S(1)} %encode_frames.1), channel_id=1, replica_groups=mesh['frame'=64,'tile'=2] {'frame'}, dimensions={0} | all-to-all | bytes 1769472 | tf_op jit(solution)/shard_map/all_to_all | solution.py:269
  65.5 1.9 %collective-permute-start.1 = (bf16[64,2,3456]{2,1,0:T(2,128)(2,1)S(1)}, bf16[64,2,3456]{2,1,0:T(2,128)(2,1)S(1)}, u32[]{:S(2)}, u32[]{:S(2)}) collective-permute-start(bf16[64,2,3456]{2,1,0:T(2,128)(2,1)S(1)} %all_to_all.10.own_ref), channel_id=1, source_target_pairs={{0,1},{1,0},{2,3},{3,2},{4,5},{5,4},{6,7},{7,6},{8,9},{9,8},{10,11... | collective-permute-start | bytes 2654216 | tf_op jit(solution)/shard_map/ppermute | solution.py:270
  67.4 0.0 copy-done.8
  67.4 0.0 copy-start.1
  67.4 2.0 %collective-permute-done.1.other_ref = bf16[64,2,3456]{2,1,0:T(2,128)(2,1)S(1)} collective-permute-done((bf16[64,2,3456]{2,1,0:T(2,128)(2,1)S(1)}, bf16[64,2,3456]{2,1,0:T(2,128)(2,1)S(1)}, u32[]{:S(2)}, u32[]{:S(2)}) %collective-permute-start.1) | collective-permute-done | bytes 884768 | tf_op jit(solution)/shard_map/ppermute | solution.py:270
  69.4 0.0 copy-done.3
  69.4 0.0 copy-done.7
  69.4 4.3 %mix_rows.1 = bf16[64,2,3456]{2,1,0:T(2,128)(2,1)S(1)} custom-call(s32[1]{0:T(128)} %bitcast.tile_ref, s32[6]{0:T(128)S(1)} %copy-done.7, s32[1,768]{1,0:T(1,128)S(1)} %broadcast_in_dim.6.slots_ref, bf16[64,2,3456]{2,1,0:T(2,128)(2,1)S(1)} %all_to_all.10.own_ref, bf16[64,2,3456]{2,1,0:T(2,128)(2,1)S(1)} %collective-permute-done.1.other_ref, ...), custom_call_target="tpu_custom_call" | custom-call | tf_op jit(solution)/shard_map/mix_rows/pallas_call | solution.py:211
  73.7 20.4 %all_to_all.11.mixed_ref = bf16[64,2,3456]{2,1,0:T(2,128)(2,1)S(1)} all-to-all(bf16[64,2,3456]{2,1,0:T(2,128)(2,1)S(1)} %mix_rows.1), channel_id=1, replica_groups=mesh['frame'=64,'tile'=2] {'frame'}, dimensions={0} | all-to-all | bytes 1769472 | tf_op jit(solution)/shard_map/all_to_all | solution.py:272
  94.2 0.0 copy-done.1
  94.2 3.8 %project_rows.1 = bf16[6,64,1792]{2,1,0:T(8,128)(2,1)} custom-call(bf16[64,2,3456]{2,1,0:T(2,128)(2,1)S(1)} %all_to_all.11.mixed_ref, bf16[1152,1792]{1,0:T(8,128)(2,1)S(1)} %copy-done.1), custom_call_target="tpu_custom_call" | custom-call | tf_op jit(solution)/shard_map/project_rows/pallas_call | solution.py:241
  (1 shorter events, 0.0 us)
Async XLA Ops:
  0.0 7.3 %copy-start.2 = (bf16[1152,1152]{1,0:T(8,128)(2,1)S(1)}, bf16[1152,1152]{1,0:T(8,128)(2,1)}, u32[]{:S(2)}) copy-start(bf16[1152,1152]{1,0:T(8,128)(2,1)} %wout_ref.1) | copy-start | bytes 7962628
  0.0 7.3 %copy-start.4 = (f32[1152]{0:T(1024)S(1)}, f32[1152]{0:T(1024)}, u32[]{:S(2)}) copy-start(f32[1152]{0:T(1024)} %gain_ref.1) | copy-start | bytes 13828
  0.0 7.3 %copy-start.5 = (f32[1152]{0:T(1024)S(1)}, f32[1152]{0:T(1024)}, u32[]{:S(2)}) copy-start(f32[1152]{0:T(1024)} %bias_ref.1) | copy-start | bytes 13828
  0.0 7.3 %copy-start.6 = (s32[64]{0:T(128)S(1)}, s32[64]{0:T(128)}, u32[]{:S(2)}) copy-start(s32[64]{0:T(128)} %param.19) | copy-start | bytes 772
  2.5 4.8 %collective-permute-start = (bf16[6,128,1152]{2,1,0:T(8,128)(2,1)S(1)}, bf16[6,128,1152]{2,1,0:T(8,128)(2,1)S(1)}, u32[]{:S(2)}, u32[]{:S(2)}) collective-permute-start(bf16[6,128,1152]{2,1,0:T(8,128)(2,1)S(1)} %get-tuple-element.5), channel_id=1, source_target_pairs={{0,1},{1,0},{2,3},{3,2},{4,5},{5,4},{6,7},{7,6},{8,9},{9,8},{10,11... | collective-permute-start | bytes 5308424 | tf_op jit(solution)/shard_map/ppermute | solution.py:263
  7.3 3.3 %copy-start = (bf16[1152,3456]{1,0:T(8,128)(2,1)S(1)}, bf16[1152,3456]{1,0:T(8,128)(2,1)}, u32[]{:S(2)}) copy-start(bf16[1152,3456]{1,0:T(8,128)(2,1)} %wqkv_ref.1) | copy-start | bytes 23887876
  38.1 29.3 %copy-start.8 = (s32[768]{0:T(1024)S(1)}, s32[768]{0:T(1024)}, u32[]{:S(2)}) copy-start(s32[768]{0:T(1024)} %param.18) | copy-start | bytes 9220
  38.1 31.4 %copy-start.3 = (f32[3,1152]{1,0:T(4,128)S(1)}, f32[3,1152]{1,0:T(4,128)}, u32[]{:S(2)}) copy-start(f32[3,1152]{1,0:T(4,128)} %taps_ref.1) | copy-start | bytes 41476
  38.1 31.4 %copy-start.7 = (s32[6]{0:T(128)S(1)}, s32[6]{0:T(128)}, u32[]{:S(2)}) copy-start(s32[6]{0:T(128)} %lengths_ref.1) | copy-start | bytes 76
  65.5 3.9 %collective-permute-start.1 = (bf16[64,2,3456]{2,1,0:T(2,128)(2,1)S(1)}, bf16[64,2,3456]{2,1,0:T(2,128)(2,1)S(1)}, u32[]{:S(2)}, u32[]{:S(2)}) collective-permute-start(bf16[64,2,3456]{2,1,0:T(2,128)(2,1)S(1)} %all_to_all.10.own_ref), channel_id=1, source_target_pairs={{0,1},{1,0},{2,3},{3,2},{4,5},{5,4},{6,7},{7,6},{8,9},{9,8},{10,11... | collective-permute-start | bytes 2654216 | tf_op jit(solution)/shard_map/ppermute | solution.py:270
  67.4 26.8 %copy-start.1 = (bf16[1152,1792]{1,0:T(8,128)(2,1)S(1)}, bf16[1152,1792]{1,0:T(8,128)(2,1)}, u32[]{:S(2)}) copy-start(bf16[1152,1792]{1,0:T(8,128)(2,1)} %w_ref.1) | copy-start | bytes 12386308

commit v2 on v1

v2 whole, which is shorter than its diff:
```python
import math

import jax
import jax.numpy as jnp
from jax import lax
from jax.experimental import pallas as pl
from jax.experimental.pallas import tpu as pltpu
from jax.sharding import PartitionSpec as P

D = 1152
HEADS = 16
HEAD_DIM = 72
PATCH = 256
HALF = 128
BLOCKS = 64
FRAMES = 384
FRAME_DEVS = 64
CLIPS = 6
FR_DEV = 6
SLOT_DEV = 12
SLOTS = 768
PAIRS = 3
PART = 640
REST = 512
OUT_CUT = 896
OUT_DEV = 1792
NORM_EPS = 1e-6
SCORE_SCALE = math.log2(math.e) / math.sqrt(HEAD_DIM)
STAGE_VMEM = 16 << 20
ENCODE_VMEM = 34 << 20
SMALL_VMEM = 16 << 20

bf16 = jnp.bfloat16
f32 = jnp.float32
NT = (((1,), (1,)), ((), ()))


def head_lanes(head):
    first, last = HEAD_DIM * head, HEAD_DIM * (head + 1) - 1
    return first // 128 * 128, (last // 128 + 1) * 128


def in_vmem(x):
    return pltpu.with_memory_space_constraint(x, pltpu.VMEM)


def in_hbm(x):
    return pltpu.with_memory_space_constraint(x, pltpu.HBM)


def normalise(rows, gain_ref, bias_ref):
    gain, bias = gain_ref[...].reshape(1, D), bias_ref[...].reshape(1, D)
    rows = rows.astype(f32)
    centred = rows - jnp.sum(rows, -1, keepdims=True) * (1.0 / D)
    variance = jnp.sum(centred * centred, -1, keepdims=True) * (1.0 / D)
    return (centred * lax.rsqrt(variance + NORM_EPS) * gain + bias).astype(bf16)


def stage_kernel(
    tile_ref, frames_any, gain_ref, bias_ref, wqkv_any, wout_any,
    own_ref, normed_ref, wqkv_ref, wout_ref, sems,
):
    rows = pl.ds(FR_DEV * tile_ref[0], FR_DEV)
    copies = [pltpu.make_async_copy(frames_any.at[rows], own_ref, sems.at[0])]
    step = D // 4
    for n in range(4):
        part = pl.ds(n * step, step)
        copies.append(pltpu.make_async_copy(wqkv_any.at[part], wqkv_ref.at[part], sems.at[n + 1]))
    copies.append(pltpu.make_async_copy(wout_any, wout_ref, sems.at[5]))
    for copy in copies:
        copy.start()
    copies[0].wait()
    for f in range(FR_DEV):
        normed_ref[f] = normalise(own_ref[f], gain_ref, bias_ref)
    for copy in copies[1:]:
        copy.wait()


def stage(tile, frames_in, gain, bias, w_qkv, w_out):
    smem, vmem, hbm = (pl.BlockSpec(memory_space=m) for m in (pltpu.SMEM, pltpu.VMEM, pltpu.HBM))
    return pl.pallas_call(
        stage_kernel,
        in_specs=[smem, hbm, vmem, vmem, hbm, hbm],
        out_specs=[vmem] * 4,
        out_shape=[
            pltpu.VMEM((FR_DEV, HALF, D), bf16),
            pltpu.VMEM((FR_DEV, HALF, D), bf16),
            pltpu.VMEM((D, 3 * D), bf16),
            pltpu.VMEM((D, D), bf16),
        ],
        scratch_shapes=[pltpu.SemaphoreType.DMA((6,))],
        compiler_params=pltpu.CompilerParams(vmem_limit_bytes=STAGE_VMEM),
        name="stage_operands",
    )(tile, in_hbm(frames_in), gain, bias, in_hbm(w_qkv), in_hbm(w_out))


def project_qkv(normed_s, w_ref, qk_s, vt_s):
    for lo in range(0, 3 * D, 256):
        hi = min(lo + 256, 3 * D)
        part = jnp.dot(normed_s[...], w_ref[:, lo:hi], preferred_element_type=f32)
        if hi <= 2 * D:
            qk_s[:, lo:hi] = part.astype(bf16)
        else:
            vt_s[lo - 2 * D : hi - 2 * D, :] = part.T.astype(bf16)


def attend(qk_s, vt_s, ctx_s):
    lane = lax.broadcasted_iota(jnp.int32, (1, D), 1)
    ones = jnp.ones((16, PATCH), bf16)

    def scores(s, head):
        lo, hi = head_lanes(head)
        start = HEAD_DIM * head
        mine = (lane[:, lo:hi] >= start) & (lane[:, lo:hi] < start + HEAD_DIM)
        rows = slice(s * PATCH, (s + 1) * PATCH)
        keys = qk_s[rows, D + lo : D + hi]
        keys = jnp.where(mine, keys, jnp.zeros_like(keys))
        return lax.dot_general(keys, qk_s[rows, lo:hi], NT, preferred_element_type=f32)

    def weigh(score):
        top = jnp.max(score, 0, keepdims=True)
        return jnp.exp2((score - top) * SCORE_SCALE).astype(bf16)

    def total(s, head, weights):
        skip = 8 * (head % 2)
        first = HEAD_DIM * head - skip
        cols = slice(s * PATCH, (s + 1) * PATCH)
        values = jnp.concatenate([vt_s[first : first + 80, cols], ones], 0)
        summed = jnp.dot(values, weights, preferred_element_type=f32)
        ctx_s[HEAD_DIM * head : HEAD_DIM * (head + 1), cols] = (
            summed[skip : skip + HEAD_DIM] / summed[80:81]
        )

    items = [(s, head) for s in range(2) for head in range(HEADS)]
    score, weights = {}, {}
    for n in range(-4, len(items)):
        if n + 4 < len(items):
            score[n + 4] = scores(*items[n + 4])
        if 0 <= n + 2 < len(items):
            weights[n + 2] = weigh(score.pop(n + 2))
        if n >= 0:
            total(*items[n], weights.pop(n))


def pooling(tile, map_ref):
    block = lax.broadcasted_iota(jnp.int32, (BLOCKS, 2 * PATCH), 0)
    col = lax.broadcasted_iota(jnp.int32, (BLOCKS, 2 * PATCH), 1)
    col_block = (col % HALF) // 4 + BLOCKS // 2 * ((col // HALF + tile) % 2)
    row = lax.broadcasted_iota(jnp.int32, (2 * BLOCKS, 1), 0)
    placing = jnp.where(map_ref[...] == row // 2, 1.0, 0.0).astype(bf16)
    member = jnp.where(block == col_block, 0.25, 0.0).astype(bf16)
    member = jnp.dot(placing, member, preferred_element_type=f32)
    frame_of = lax.broadcasted_iota(jnp.int32, (1, 2 * PATCH), 1) // PATCH
    return jnp.where(frame_of == row % 2, member, 0.0).astype(bf16)


def encode_kernel(
    tile_ref, own_ref, own_normed, other_ref, gain_ref, bias_ref, wqkv_ref, wout_ref, map_ref, out_ref,
    normed_s, qk_s, vt_s, ctx_s, pooled_x, pooled_ctx, pool_s,
):
    pool_s[...] = pooling(tile_ref[0], map_ref)

    def one_pair(pair, carry):
        for s in range(2):
            frame = 2 * pair + s
            mid = s * PATCH + HALF
            normed_s[s * PATCH : mid, :] = own_normed[frame]
            normed_s[mid : (s + 1) * PATCH, :] = normalise(other_ref[frame], gain_ref, bias_ref)
        project_qkv(normed_s, wqkv_ref, qk_s, vt_s)
        attend(qk_s, vt_s, ctx_s)
        rows = pl.ds(pl.multiple_of(pair * 2 * BLOCKS, 2 * BLOCKS), 2 * BLOCKS)
        pooled = lax.dot_general(
            pool_s[...], ctx_s[...].astype(bf16), NT, preferred_element_type=f32
        )
        pooled_ctx[rows, :] = pooled.astype(bf16)
        patches = [ref[2 * pair + s] for s in range(2) for ref in (own_ref, other_ref)]
        patches = jnp.concatenate(patches, 0)
        pooled_x[rows, :] = jnp.dot(pool_s[...], patches, preferred_element_type=f32)
        return carry

    lax.fori_loop(0, PAIRS, one_pair, 0)
    for pair in range(PAIRS):
        rows = slice(pair * 2 * BLOCKS, (pair + 1) * 2 * BLOCKS)
        total = jnp.dot(pooled_ctx[rows, :], wout_ref[...], preferred_element_type=f32)
        total = (total + pooled_x[rows, :]).astype(bf16)
        out_ref[:, :, pair * D : (pair + 1) * D] = total.reshape(BLOCKS, 2, D)


def encode(tile, own, own_normed, other, gain, bias, w_qkv, w_out, block_map):
    vmem = pl.BlockSpec(memory_space=pltpu.VMEM)
    return pl.pallas_call(
        encode_kernel,
        in_specs=[pl.BlockSpec(memory_space=pltpu.SMEM)] + [vmem] * 8,
        out_specs=vmem,
        out_shape=pltpu.VMEM((BLOCKS, 2, PAIRS * D), bf16),
        scratch_shapes=[
            pltpu.VMEM((2 * PATCH, D), bf16),
            pltpu.VMEM((2 * PATCH, 2 * D), bf16),
            pltpu.VMEM((D, 2 * PATCH), bf16),
            pltpu.VMEM((D, 2 * PATCH), f32),
            pltpu.VMEM((PAIRS * 2 * BLOCKS, D), f32),
            pltpu.VMEM((PAIRS * 2 * BLOCKS, D), bf16),
            pltpu.VMEM((2 * BLOCKS, 2 * PATCH), bf16),
        ],
        compiler_params=pltpu.CompilerParams(vmem_limit_bytes=ENCODE_VMEM),
        name="encode_frames",
    )(
        tile, in_vmem(own), in_vmem(own_normed), in_vmem(other), gain, bias,
        in_vmem(w_qkv), in_vmem(w_out), block_map,
    )


def own_rows(ref, rows_s, tile):
    for j in range(PAIRS):
        cols = pl.ds(pl.multiple_of(j * D + 512 * tile, 128), PART)
        rows_s[j * 128 : (j + 1) * 128, :] = ref[:, :, cols].reshape(128, PART)


def pick_kernel(
    tile_ref, lengths_ref, slots_ref, own_ref, other_hit, picked_ref, rows_s, own_hit
):
    tile = tile_ref[0]
    own_rows(own_ref, rows_s, tile)
    code = slots_ref[...] + 1
    code = jnp.concatenate([code // 16, code % 16] + [jnp.zeros_like(code)] * 6, 0)
    slot = lax.broadcasted_iota(jnp.int32, (SLOTS, SLOTS), 0)
    col = lax.broadcasted_iota(jnp.int32, (1, SLOTS), 1)
    group, place = col // 128, col % 128
    core = (group // PAIRS + tile) % 2
    source = SLOT_DEV * (place // 2) + FR_DEV * core + 2 * (group % PAIRS) + place % 2
    moved = jnp.where(slot == source, 1.0, 0.0).astype(bf16)
    code = jnp.dot(code.astype(f32).astype(bf16), moved, preferred_element_type=f32)
    held = (code[0:1] * 16.0 + code[1:2]).astype(jnp.int32) - 1
    row = lax.broadcasted_iota(jnp.int32, (128, 1), 0)
    for step in range(PAIRS):
        frame = FR_DEV * (row // 2) + 2 * step + row % 2
        first, last = frame < 0, frame + 1 == FRAMES
        start = 0
        for c in range(CLIPS):
            first |= frame == start
            last |= frame + 1 == start
            start += lengths_ref[c]
        wanted = (jnp.where(first, -2, frame - 1), frame, jnp.where(last, -2, frame + 1))
        for tap, want in enumerate(wanted):
            rows = slice((PAIRS * step + tap) * 128, (PAIRS * step + tap + 1) * 128)
            hit = jnp.where(held == want, 1.0, 0.0).astype(bf16)
            own_hit[rows, :] = hit[:, : SLOTS // 2]
            other_hit[rows, :] = hit[:, SLOTS // 2 :]
    picked_ref[...] = jnp.dot(own_hit[...], rows_s[...], preferred_element_type=f32)


def pick(tile, lengths, slots, own):
    smem, vmem = (pl.BlockSpec(memory_space=m) for m in (pltpu.SMEM, pltpu.VMEM))
    return pl.pallas_call(
        pick_kernel,
        in_specs=[smem, smem, vmem, vmem],
        out_specs=[vmem, vmem],
        out_shape=[
            pltpu.VMEM((9 * 128, SLOTS // 2), bf16),
            pltpu.VMEM((9 * 128, PART), f32),
        ],
        scratch_shapes=[
            pltpu.VMEM((SLOTS // 2, PART), bf16),
            pltpu.VMEM((9 * 128, SLOTS // 2), bf16),
        ],
        compiler_params=pltpu.CompilerParams(vmem_limit_bytes=SMALL_VMEM),
        name="pick_own_rows",
    )(tile, lengths, slots, in_vmem(own))


def mix_kernel(tile_ref, other_ref, other_hit, picked_ref, taps_ref, out_ref, rows_s, picked_s):
    tile = tile_ref[0]
    own_rows(other_ref, rows_s, tile)
    picked_s[...] = jnp.dot(other_hit[...], rows_s[...], preferred_element_type=f32)
    taps = taps_ref[:, pl.ds(pl.multiple_of(512 * tile, 128), PART)]
    for step in range(PAIRS):
        mixed = 0.0
        for tap in range(3):
            first = (PAIRS * step + tap) * 128
            rows = slice(first, first + 128)
            mixed += taps[tap : tap + 1] * (picked_s[rows, :] + picked_ref[rows, :])
        mixed = mixed.astype(bf16).reshape(FRAME_DEVS, 2, PART)
        out_ref[:, :, step * PART : (step + 1) * PART] = mixed


def mix(tile, other, other_hit, picked, taps):
    smem, vmem = (pl.BlockSpec(memory_space=m) for m in (pltpu.SMEM, pltpu.VMEM))
    return pl.pallas_call(
        mix_kernel,
        in_specs=[smem, vmem, vmem, vmem, vmem],
        out_specs=vmem,
        out_shape=pltpu.VMEM((FRAME_DEVS, 2, PAIRS * PART), bf16),
        scratch_shapes=[
            pltpu.VMEM((SLOTS // 2, PART), bf16),
            pltpu.VMEM((9 * 128, PART), f32),
        ],
        compiler_params=pltpu.CompilerParams(vmem_limit_bytes=SMALL_VMEM),
        name="mix_rows",
    )(tile, in_vmem(other), in_vmem(other_hit), in_vmem(picked), taps)


def deinterleave(rows):
    row = lax.broadcasted_iota(jnp.int32, (128, 128), 0)
    col = lax.broadcasted_iota(jnp.int32, (128, 128), 1)
    order = jnp.where(col == 2 * (row % BLOCKS) + row // BLOCKS, 1.0, 0.0).astype(bf16)
    return jnp.dot(order, rows, preferred_element_type=f32).astype(bf16)


def project_own_kernel(tile_ref, own_ref, w_ref, part_ref, rows_s):
    for j in range(PAIRS):
        rows = own_ref[:, :, j * PART : (j + 1) * PART].reshape(128, PART)
        rows_s[j * 128 : (j + 1) * 128, :] = deinterleave(rows)
    first = pl.multiple_of(512 * tile_ref[0], 128)
    for lo in range(0, OUT_DEV, 256):
        weights = w_ref[pl.ds(first, PART), lo : lo + 256]
        part_ref[:, lo : lo + 256] = jnp.dot(rows_s[...], weights, preferred_element_type=f32)


def project_own(tile, own, w_proj):
    smem, vmem = (pl.BlockSpec(memory_space=m) for m in (pltpu.SMEM, pltpu.VMEM))
    return pl.pallas_call(
        project_own_kernel,
        in_specs=[smem, vmem, vmem],
        out_specs=vmem,
        out_shape=pltpu.VMEM((FR_DEV * BLOCKS, OUT_DEV), f32),
        scratch_shapes=[pltpu.VMEM((FR_DEV * BLOCKS, PART), bf16)],
        compiler_params=pltpu.CompilerParams(vmem_limit_bytes=SMALL_VMEM),
        name="project_own_channels",
    )(tile, in_vmem(own), in_vmem(w_proj))


def project_kernel(tile_ref, other_ref, part_ref, w_ref, out_hbm, rows_s, out_s, sems):
    tile = tile_ref[0]
    for j in range(PAIRS):
        cols = pl.ds(pl.multiple_of(j * PART + 128 * (1 - tile), 128), REST)
        rows_s[j * 128 : (j + 1) * 128, :] = deinterleave(other_ref[:, :, cols].reshape(128, REST))
    first = pl.multiple_of(PART * (1 - tile), 128)
    copies = []
    for n, lo in enumerate(range(0, OUT_DEV, OUT_CUT)):
        for mid in range(lo, lo + OUT_CUT, 256):
            cols = slice(mid, min(mid + 256, lo + OUT_CUT))
            weights = w_ref[pl.ds(first, REST), cols]
            out = jnp.dot(rows_s[...], weights, preferred_element_type=f32) + part_ref[:, cols]
            out_s[:, :, cols] = out.astype(bf16).reshape(FR_DEV, BLOCKS, cols.stop - cols.start)
        cols = pl.ds(lo, OUT_CUT)
        copies.append(
            pltpu.make_async_copy(out_s.at[:, :, cols], out_hbm.at[:, :, cols], sems.at[n])
        )
        copies[n].start()
    for copy in copies:
        copy.wait()


def project(tile, other, part, w_proj):
    smem, vmem = (pl.BlockSpec(memory_space=m) for m in (pltpu.SMEM, pltpu.VMEM))
    shape = (FR_DEV, BLOCKS, OUT_DEV)
    return pl.pallas_call(
        project_kernel,
        in_specs=[smem, vmem, vmem, vmem],
        out_specs=pl.BlockSpec(memory_space=pltpu.HBM),
        out_shape=jax.ShapeDtypeStruct(shape, bf16),
        scratch_shapes=[
            pltpu.VMEM((FR_DEV * BLOCKS, REST), bf16),
            pltpu.VMEM(shape, bf16),
            pltpu.SemaphoreType.DMA((OUT_DEV // OUT_CUT,)),
        ],
        compiler_params=pltpu.CompilerParams(vmem_limit_bytes=SMALL_VMEM),
        name="project_rows",
    )(tile, in_vmem(other), in_vmem(part), in_vmem(w_proj))


SWAP = [(0, 1), (1, 0)]


def on_device(
    frames_in, norm_gain, norm_bias, w_qkv, w_out, time_taps, w_proj, clip_lengths, frame_slot, block_map
):
    tile = lax.axis_index("tile")
    sent = lax.dynamic_slice_in_dim(frames_in, FR_DEV * (1 - tile), FR_DEV)
    other = lax.ppermute(sent, "tile", SWAP)
    core = jnp.reshape(tile, (1,)).astype(jnp.int32)
    core = jnp.reshape(tile, (1,)).astype(jnp.int32)
    frames_in, _ = lax.optimization_barrier((frames_in, sent))
    own, own_normed, w_qkv, w_out = stage(core, frames_in, norm_gain, norm_bias, w_qkv, w_out)
    pooled = encode(
        core, own, own_normed, other, norm_gain, norm_bias, w_qkv, w_out, block_map[None]
    )
    spread = lax.all_to_all(pooled, "frame", split_axis=0, concat_axis=0, tiled=True)
    spread_other = lax.ppermute(spread, "tile", SWAP)
    other_hit, picked = pick(core, clip_lengths, frame_slot[None], spread)
    mixed = mix(core, spread_other, other_hit, picked, time_taps)
    home = lax.all_to_all(mixed, "frame", split_axis=0, concat_axis=0, tiled=True)
    home_other = lax.ppermute(home, "tile", SWAP)
    part = project_own(core, home, w_proj)
    return project(core, home_other, part, w_proj)


def solution(mesh):
    in_specs = (P("frame", "tile", None), P(), P(), P(), P(), P(), P(None, "tile"), P(), P(), P())
    return jax.shard_map(
        on_device, mesh=mesh, in_specs=in_specs, out_specs=P("frame", None, "tile"), check_vma=False
    )
```

time: 98.7 us -> 89.3 us (0.905)
  waiting for transfers between devices: 5.36 us -> 0.03 us
  local copies, waits for them, and re-layouts: 5.74 us -> 1.68 us
  blocking collectives: 47.9 us -> 44.2 us
  Pallas kernels: 35.6 us -> 38.2 us
  starting transfers between devices: 3.35 us -> 4.71 us
    all_to_all x1, blocking collectives: 20.4 us -> 16.6 us  [on_device(): lax.all_to_all(mixed, 'frame', split_axis=0, concat_axis=0, tiled=True)]
    pallas_call x2 -> x5, Pallas kernels: 8.09 us -> 11.5 us  [the longest x1 4.67 us: stage(): pl.pallas_call(stage_kernel, in_specs=[smem, hbm, vmem, vmem, hbm, hbm],...]
    ppermute x1, waiting for transfers between devices: 3.32 us -> 0.01 us  [on_device(): other = lax.ppermute(sent, 'tile', SWAP)]
    unnamed x18 -> x14, local copies, waits for them, and re-layouts: 3.29 us -> 0.04 us
    ppermute x1, waiting for transfers between devices: 2.04 us -> 0.01 us  [on_device(): spread_other = lax.ppermute(spread, 'tile', SWAP)]
    ppermute x0 -> x1, starting transfers between devices: none -> 1.65 us  [on_device(): home_other = lax.ppermute(home, 'tile', SWAP)]
  transfers between devices with their start and end apart: 2 -> 3, of which waited for: 2 -> 0; matrix products, arithmetic and copies ran while one was open for 0% -> 0% of each run, Pallas kernels for 0% -> 9%
where the time goes in v2:
time: 89.3 us; the launch traced here: 89.1 us
  blocking collectives  44.2 us (49%)
  Pallas kernels  38.2 us (43%)
  starting transfers between devices  4.71 us (5%)
  local copies, waits for them, and re-layouts  1.68 us (2%)
    all_to_all x1, blocking collectives, on_device(): lax.all_to_all(pooled, 'frame', split_axis=0, concat_axis=0, tiled=True)  27.6 us
    pallas_call x1, Pallas kernels, encode(): pl.pallas_call(encode_kernel, in_specs=[pl.BlockSpec(memory_space=pltpu.S...  26.7 us
    all_to_all x1, blocking collectives, on_device(): lax.all_to_all(mixed, 'frame', split_axis=0, concat_axis=0, tiled=True)  16.6 us
    pallas_call x1, Pallas kernels, stage(): pl.pallas_call(stage_kernel, in_specs=[smem, hbm, vmem, vmem, hbm, hbm],...  4.67 us
    pallas_call x1, Pallas kernels, pick(): pl.pallas_call(pick_kernel, in_specs=[smem, smem, vmem, vmem], out_specs=...  2.16 us
    pallas_call x1, Pallas kernels, project(): pl.pallas_call(project_kernel, in_specs=[smem, vmem, vmem, vmem], out_spe...  1.97 us
  transfers between devices with their start and end apart: 3, of which 0 were waited for; matrix products, arithmetic and copies ran while one was open for 0% of the time, Pallas kernels for 9%

profile of v2, /device:TPU:1, one launch (start us, length us, event | category | flops | bytes accessed | tf_op | source)
XLA Modules:
  0.0 89.1 jit_solution(4299932169267412274)
XLA Ops:
  0.0 0.0 copy-start.2
  0.0 0.0 copy-start.1
  0.0 1.6 %constant_dynamic-slice_fusion = bf16[6,128,1152]{2,1,0:T(8,128)(2,1)S(1)} fusion(bf16[12,128,1152]{2,1,0:T(8,128)(2,1)} %frames_any, s32[]{:T(128)S(6)} %select_n.3), kind=kLoop, calls=%fused_computation | loop fusion | bytes 3538948 | tf_op jit(solution)/shard_map/dynamic_slice | solution.py:379
  1.6 1.5 %collective-permute-start = (bf16[6,128,1152]{2,1,0:T(8,128)(2,1)S(1)}, bf16[6,128,1152]{2,1,0:T(8,128)(2,1)S(1)}, u32[]{:S(2)}, u32[]{:S(2)}) collective-permute-start(bf16[6,128,1152]{2,1,0:T(8,128)(2,1)S(1)} %constant_dynamic-slice_fusion), channel_id=1, source_target_pairs={{0,1},{1,0},{2,3},{3,2},{4,5},{5,4},{6,7},{7,6},{8,9},{9,8},{10,11... | collective-permute-start | bytes 5308424 | tf_op jit(solution)/shard_map/ppermute | solution.py:380
  3.1 0.0 copy-done.2
  3.2 0.0 copy-done.1
  3.2 0.0 copy-start.4
  3.2 4.7 %stage_operands.1 = (bf16[6,128,1152]{2,1,0:T(8,128)(2,1)S(1)}, bf16[6,128,1152]{2,1,0:T(8,128)(2,1)S(1)}, bf16[1152,3456]{1,0:T(8,128)(2,1)S(1)}, bf16[1152,1152]{1,0:T(8,128)(2,1)S(1)}) custom-call(s32[1]{0:T(128)} %bitcast.tile_ref, bf16[12,128,1152]{2,1,0:T(8,128)(2,1)} %frames_any, f32[1152]{0:T(1024)S(1)} %copy-done.1, f32[1152]{0:T(1024)S(1)} %copy-done.2, ...), custom_call_target="tpu_custom_call" | custom-call | tf_op jit(solution)/shard_map/stage_operands/pallas_call | solution.py:81
  7.8 0.0 collective-permute-done.other_ref
  7.8 0.0 copy-done.4
  7.9 0.0 copy-start.6
  7.9 0.0 copy-start.5
  7.9 26.7 %encode_frames.1 = bf16[64,2,3456]{2,1,0:T(2,128)(2,1)S(1)} custom-call(s32[1]{0:T(128)} %bitcast.tile_ref, bf16[6,128,1152]{2,1,0:T(8,128)(2,1)S(1)} %get-tuple-element.13.own_ref, bf16[6,128,1152]{2,1,0:T(8,128)(2,1)S(1)} %get-tuple-element.14.own_normed, bf16[6,128,1152]{2,1,0:T(8,128)(2,1)S(1)} %collective-permute-done.other_ref, f32[1152]{0:T(1024)S(1)} %copy-done.1, ...), custom_call_target="tpu_custom_call" | custom-call | tf_op jit(solution)/shard_map/encode_frames/pallas_call | solution.py:191
  34.6 0.0 copy-start.3
  34.6 27.6 %all_to_all.10.own_ref = bf16[64,2,3456]{2,1,0:T(2,128)(2,1)S(1)} all-to-all(bf16[64,2,3456]{2,1,0:T(2,128)(2,1)S(1)} %encode_frames.1), channel_id=1, replica_groups=mesh['frame'=64,'tile'=2] {'frame'}, dimensions={0} | all-to-all | bytes 1769472 | tf_op jit(solution)/shard_map/all_to_all | solution.py:388
  62.2 1.6 %collective-permute-start.1 = (bf16[64,2,3456]{2,1,0:T(2,128)(2,1)S(1)}, bf16[64,2,3456]{2,1,0:T(2,128)(2,1)S(1)}, u32[]{:S(2)}, u32[]{:S(2)}) collective-permute-start(bf16[64,2,3456]{2,1,0:T(2,128)(2,1)S(1)} %all_to_all.10.own_ref), channel_id=1, source_target_pairs={{0,1},{1,0},{2,3},{3,2},{4,5},{5,4},{6,7},{7,6},{8,9},{9,8},{10,11... | collective-permute-start | bytes 2654216 | tf_op jit(solution)/shard_map/ppermute | solution.py:389
  63.7 0.0 copy-done.6
  63.7 0.0 copy-done.5
  63.7 2.2 %pick_own_rows.1 = (bf16[1152,384]{1,0:T(8,128)(2,1)S(1)}, f32[1152,640]{1,0:T(8,128)S(1)}) custom-call(s32[1]{0:T(128)} %bitcast.tile_ref, s32[6]{0:T(128)S(1)} %copy-done.5, s32[1,768]{1,0:T(1,128)S(1)} %broadcast_in_dim.7.slots_ref, bf16[64,2,3456]{2,1,0:T(2,128)(2,1)S(1)} %all_to_all.10.own_ref), custom_call_target="tpu_custom_call" | custom-call | tf_op jit(solution)/shard_map/pick_own_rows/pallas_call | solution.py:254
  65.9 0.0 collective-permute-done.1.other_ref
  65.9 0.0 copy-done.3
  65.9 0.0 copy-start
  65.9 1.2 %mix_rows.1 = bf16[64,2,1920]{2,1,0:T(2,128)(2,1)S(1)} custom-call(s32[1]{0:T(128)} %bitcast.tile_ref, bf16[64,2,3456]{2,1,0:T(2,128)(2,1)S(1)} %collective-permute-done.1.other_ref, bf16[1152,384]{1,0:T(8,128)(2,1)S(1)} %get-tuple-element.17.other_hit, f32[1152,640]{1,0:T(8,128)S(1)} %get-tuple-element.18.picked_ref, f32[3,1152]{1,0:T(4,128)S(1)} %copy-done.3), custom_call_target="tpu_custom_call" | custom-call | tf_op jit(solution)/shard_map/mix_rows/pallas_call | solution.py:288
  67.1 16.6 %all_to_all.11.own_ref = bf16[64,2,1920]{2,1,0:T(2,128)(2,1)S(1)} all-to-all(bf16[64,2,1920]{2,1,0:T(2,128)(2,1)S(1)} %mix_rows.1), channel_id=1, replica_groups=mesh['frame'=64,'tile'=2] {'frame'}, dimensions={0} | all-to-all | bytes 983040 | tf_op jit(solution)/shard_map/all_to_all | solution.py:392
  83.8 1.7 %collective-permute-start.2 = (bf16[64,2,1920]{2,1,0:T(2,128)(2,1)S(1)}, bf16[64,2,1920]{2,1,0:T(2,128)(2,1)S(1)}, u32[]{:S(2)}, u32[]{:S(2)}) collective-permute-start(bf16[64,2,1920]{2,1,0:T(2,128)(2,1)S(1)} %all_to_all.11.own_ref), channel_id=1, source_target_pairs={{0,1},{1,0},{2,3},{3,2},{4,5},{5,4},{6,7},{7,6},{8,9},{9,8},{10,11... | collective-permute-start | bytes 1474568 | tf_op jit(solution)/shard_map/ppermute | solution.py:393
  85.4 0.0 copy-done
  85.4 1.5 %project_own_channels.1.part_ref = f32[384,1792]{1,0:T(8,128)S(1)} custom-call(s32[1]{0:T(128)} %bitcast.tile_ref, bf16[64,2,1920]{2,1,0:T(2,128)(2,1)S(1)} %all_to_all.11.own_ref, bf16[1152,1792]{1,0:T(8,128)(2,1)S(1)} %copy-done), custom_call_target="tpu_custom_call" | custom-call | tf_op jit(solution)/shard_map/project_own_channels/pallas_call | solution.py:321
  86.9 0.0 collective-permute-done.2.other_ref
  86.9 2.0 %project_rows.1 = bf16[6,64,1792]{2,1,0:T(8,128)(2,1)} custom-call(s32[1]{0:T(128)} %bitcast.tile_ref, bf16[64,2,1920]{2,1,0:T(2,128)(2,1)S(1)} %collective-permute-done.2.other_ref, f32[384,1792]{1,0:T(8,128)S(1)} %project_own_channels.1.part_ref, bf16[1152,1792]{1,0:T(8,128)(2,1)S(1)} %copy-done), custom_call_target="tpu_custom_call" | custom-call | tf_op jit(solution)/shard_map/project_rows/pallas_call | solution.py:357
  (1 shorter events, 0.0 us)
Async XLA Ops:
  0.0 3.2 %copy-start.2 = (f32[1152]{0:T(1024)S(1)}, f32[1152]{0:T(1024)}, u32[]{:S(2)}) copy-start(f32[1152]{0:T(1024)} %bias_ref.3) | copy-start | bytes 13828
  0.0 3.2 %copy-start.1 = (f32[1152]{0:T(1024)S(1)}, f32[1152]{0:T(1024)}, u32[]{:S(2)}) copy-start(f32[1152]{0:T(1024)} %gain_ref.3) | copy-start | bytes 13828
  1.6 6.2 %collective-permute-start = (bf16[6,128,1152]{2,1,0:T(8,128)(2,1)S(1)}, bf16[6,128,1152]{2,1,0:T(8,128)(2,1)S(1)}, u32[]{:S(2)}, u32[]{:S(2)}) collective-permute-start(bf16[6,128,1152]{2,1,0:T(8,128)(2,1)S(1)} %constant_dynamic-slice_fusion), channel_id=1, source_target_pairs={{0,1},{1,0},{2,3},{3,2},{4,5},{5,4},{6,7},{7,6},{8,9},{9,8},{10,11... | collective-permute-start | bytes 5308424 | tf_op jit(solution)/shard_map/ppermute | solution.py:380
  3.2 4.7 %copy-start.4 = (s32[64]{0:T(128)S(1)}, s32[64]{0:T(128)}, u32[]{:S(2)}) copy-start(s32[64]{0:T(128)} %param.19) | copy-start | bytes 772
  7.9 55.9 %copy-start.6 = (s32[768]{0:T(1024)S(1)}, s32[768]{0:T(1024)}, u32[]{:S(2)}) copy-start(s32[768]{0:T(1024)} %param.18) | copy-start | bytes 9220
  7.9 55.9 %copy-start.5 = (s32[6]{0:T(128)S(1)}, s32[6]{0:T(128)}, u32[]{:S(2)}) copy-start(s32[6]{0:T(128)} %lengths_ref.1) | copy-start | bytes 76
  34.6 31.3 %copy-start.3 = (f32[3,1152]{1,0:T(4,128)S(1)}, f32[3,1152]{1,0:T(4,128)}, u32[]{:S(2)}) copy-start(f32[3,1152]{1,0:T(4,128)} %taps_ref.1) | copy-start | bytes 41476
  62.2 3.7 %collective-permute-start.1 = (bf16[64,2,3456]{2,1,0:T(2,128)(2,1)S(1)}, bf16[64,2,3456]{2,1,0:T(2,128)(2,1)S(1)}, u32[]{:S(2)}, u32[]{:S(2)}) collective-permute-start(bf16[64,2,3456]{2,1,0:T(2,128)(2,1)S(1)} %all_to_all.10.own_ref), channel_id=1, source_target_pairs={{0,1},{1,0},{2,3},{3,2},{4,5},{5,4},{6,7},{7,6},{8,9},{9,8},{10,11... | collective-permute-start | bytes 2654216 | tf_op jit(solution)/shard_map/ppermute | solution.py:389
  65.9 19.5 %copy-start = (bf16[1152,1792]{1,0:T(8,128)(2,1)S(1)}, bf16[1152,1792]{1,0:T(8,128)(2,1)}, u32[]{:S(2)}) copy-start(bf16[1152,1792]{1,0:T(8,128)(2,1)} %w_ref.3) | copy-start | bytes 12386308
  83.8 3.1 %collective-permute-start.2 = (bf16[64,2,1920]{2,1,0:T(2,128)(2,1)S(1)}, bf16[64,2,1920]{2,1,0:T(2,128)(2,1)S(1)}, u32[]{:S(2)}, u32[]{:S(2)}) collective-permute-start(bf16[64,2,1920]{2,1,0:T(2,128)(2,1)S(1)} %all_to_all.11.own_ref), channel_id=1, source_target_pairs={{0,1},{1,0},{2,3},{3,2},{4,5},{5,4},{6,7},{7,6},{8,9},{9,8},{10,11... | collective-permute-start | bytes 1474568 | tf_op jit(solution)/shard_map/ppermute | solution.py:393

commit v3 on v2

--- a/solution.py
+++ b/solution.py
@@ -56,19 +56,43 @@
     return (centred * lax.rsqrt(variance + NORM_EPS) * gain + bias).astype(bf16)
 
 
+def cut_kernel(tile_ref, frames_hbm, out_ref, sems):
+    first = FR_DEV * (1 - tile_ref[0])
+    copies = []
+    for f in range(FR_DEV):
+        copies.append(
+            pltpu.make_async_copy(frames_hbm.at[first + f], out_ref.at[f], sems.at[f])
+        )
+        copies[f].start()
+    for copy in copies:
+        copy.wait()
+
+
+def cut_sent(tile, frames_in):
+    return pl.pallas_call(
+        cut_kernel,
+        in_specs=[pl.BlockSpec(memory_space=m) for m in (pltpu.SMEM, pltpu.HBM)],
+        out_specs=pl.BlockSpec(memory_space=pltpu.VMEM),
+        out_shape=pltpu.VMEM((FR_DEV, HALF, D), bf16),
+        scratch_shapes=[pltpu.SemaphoreType.DMA((FR_DEV,))],
+        compiler_params=pltpu.CompilerParams(vmem_limit_bytes=STAGE_VMEM),
+        name="cut_sent_half",
+    )(tile, in_hbm(frames_in))
+
+
 def stage_kernel(
-    tile_ref, frames_any, gain_ref, bias_ref, wqkv_any, wout_any,
-    own_ref, normed_ref, wqkv_ref, wout_ref, sems,
+    tile_ref, frames_hbm, gain_ref, bias_ref, map_ref, wqkv_hbm,
+    own_ref, normed_ref, wqkv_ref, pool_ref, sems,
 ):
     rows = pl.ds(FR_DEV * tile_ref[0], FR_DEV)
-    copies = [pltpu.make_async_copy(frames_any.at[rows], own_ref, sems.at[0])]
+    copies = [pltpu.make_async_copy(frames_hbm.at[rows], own_ref, sems.at[0])]
     step = D // 4
     for n in range(4):
         part = pl.ds(n * step, step)
-        copies.append(pltpu.make_async_copy(wqkv_any.at[part], wqkv_ref.at[part], sems.at[n + 1]))
-    copies.append(pltpu.make_async_copy(wout_any, wout_ref, sems.at[5]))
+        copies.append(pltpu.make_async_copy(wqkv_hbm.at[part], wqkv_ref.at[part], sems.at[n + 1]))
     for copy in copies:
         copy.start()
+    pool_ref[...] = pooling(tile_ref[0], map_ref)
     copies[0].wait()
     for f in range(FR_DEV):
         normed_ref[f] = normalise(own_ref[f], gain_ref, bias_ref)
@@ -76,22 +100,22 @@
         copy.wait()
 
 
-def stage(tile, frames_in, gain, bias, w_qkv, w_out):
+def stage(tile, frames_in, gain, bias, block_map, w_qkv):
     smem, vmem, hbm = (pl.BlockSpec(memory_space=m) for m in (pltpu.SMEM, pltpu.VMEM, pltpu.HBM))
     return pl.pallas_call(
         stage_kernel,
-        in_specs=[smem, hbm, vmem, vmem, hbm, hbm],
+        in_specs=[smem, hbm, vmem, vmem, vmem, hbm],
         out_specs=[vmem] * 4,
         out_shape=[
             pltpu.VMEM((FR_DEV, HALF, D), bf16),
             pltpu.VMEM((FR_DEV, HALF, D), bf16),
             pltpu.VMEM((D, 3 * D), bf16),
-            pltpu.VMEM((D, D), bf16),
-        ],
-        scratch_shapes=[pltpu.SemaphoreType.DMA((6,))],
+            pltpu.VMEM((2 * BLOCKS, 2 * PATCH), bf16),
+        ],
+        scratch_shapes=[pltpu.SemaphoreType.DMA((5,))],
         compiler_params=pltpu.CompilerParams(vmem_limit_bytes=STAGE_VMEM),
         name="stage_operands",
-    )(tile, in_hbm(frames_in), gain, bias, in_hbm(w_qkv), in_hbm(w_out))
+    )(tile, in_hbm(frames_in), gain, bias, block_map, in_hbm(w_qkv))
 
 
 def project_qkv(normed_s, w_ref, qk_s, vt_s):
@@ -101,7 +125,7 @@
         if hi <= 2 * D:
             qk_s[:, lo:hi] = part.astype(bf16)
         else:
-            vt_s[lo - 2 * D : hi - 2 * D, :] = part.T.astype(bf16)
+            vt_s[lo - 2 * D : hi - 2 * D, :] = part.astype(bf16).T
 
 
 def attend(qk_s, vt_s, ctx_s):
@@ -133,11 +157,11 @@
 
     items = [(s, head) for s in range(2) for head in range(HEADS)]
     score, weights = {}, {}
-    for n in range(-4, len(items)):
-        if n + 4 < len(items):
-            score[n + 4] = scores(*items[n + 4])
-        if 0 <= n + 2 < len(items):
-            weights[n + 2] = weigh(score.pop(n + 2))
+    for n in range(-6, len(items)):
+        if n + 6 < len(items):
+            score[n + 6] = scores(*items[n + 6])
+        if 0 <= n + 3 < len(items):
+            weights[n + 3] = weigh(score.pop(n + 3))
         if n >= 0:
             total(*items[n], weights.pop(n))
 
@@ -155,10 +179,11 @@
 
 
 def encode_kernel(
-    tile_ref, own_ref, own_normed, other_ref, gain_ref, bias_ref, wqkv_ref, wout_ref, map_ref, out_ref,
-    normed_s, qk_s, vt_s, ctx_s, pooled_x, pooled_ctx, pool_s,
+    own_ref, own_normed, other_ref, gain_ref, bias_ref, wqkv_ref, wout_hbm, pool_ref, out_ref,
+    wout_s, normed_s, qk_s, vt_s, ctx_s, pooled_x, pooled_ctx, sem,
 ):
-    pool_s[...] = pooling(tile_ref[0], map_ref)
+    wout_copy = pltpu.make_async_copy(wout_hbm, wout_s, sem)
+    wout_copy.start()
 
     def one_pair(pair, carry):
         for s in range(2):
@@ -170,43 +195,45 @@
         attend(qk_s, vt_s, ctx_s)
         rows = pl.ds(pl.multiple_of(pair * 2 * BLOCKS, 2 * BLOCKS), 2 * BLOCKS)
         pooled = lax.dot_general(
-            pool_s[...], ctx_s[...].astype(bf16), NT, preferred_element_type=f32
+            pool_ref[...], ctx_s[...].astype(bf16), NT, preferred_element_type=f32
         )
         pooled_ctx[rows, :] = pooled.astype(bf16)
         patches = [ref[2 * pair + s] for s in range(2) for ref in (own_ref, other_ref)]
         patches = jnp.concatenate(patches, 0)
-        pooled_x[rows, :] = jnp.dot(pool_s[...], patches, preferred_element_type=f32)
+        pooled_x[rows, :] = jnp.dot(pool_ref[...], patches, preferred_element_type=f32)
         return carry
 
     lax.fori_loop(0, PAIRS, one_pair, 0)
+    wout_copy.wait()
     for pair in range(PAIRS):
         rows = slice(pair * 2 * BLOCKS, (pair + 1) * 2 * BLOCKS)
-        total = jnp.dot(pooled_ctx[rows, :], wout_ref[...], preferred_element_type=f32)
+        total = jnp.dot(pooled_ctx[rows, :], wout_s[...], preferred_element_type=f32)
         total = (total + pooled_x[rows, :]).astype(bf16)
         out_ref[:, :, pair * D : (pair + 1) * D] = total.reshape(BLOCKS, 2, D)
 
 
-def encode(tile, own, own_normed, other, gain, bias, w_qkv, w_out, block_map):
-    vmem = pl.BlockSpec(memory_space=pltpu.VMEM)
+def encode(own, own_normed, other, gain, bias, w_qkv, w_out, pool):
+    vmem, hbm = (pl.BlockSpec(memory_space=m) for m in (pltpu.VMEM, pltpu.HBM))
     return pl.pallas_call(
         encode_kernel,
-        in_specs=[pl.BlockSpec(memory_space=pltpu.SMEM)] + [vmem] * 8,
+        in_specs=[vmem] * 6 + [hbm, vmem],
         out_specs=vmem,
         out_shape=pltpu.VMEM((BLOCKS, 2, PAIRS * D), bf16),
         scratch_shapes=[
+            pltpu.VMEM((D, D), bf16),
             pltpu.VMEM((2 * PATCH, D), bf16),
             pltpu.VMEM((2 * PATCH, 2 * D), bf16),
             pltpu.VMEM((D, 2 * PATCH), bf16),
             pltpu.VMEM((D, 2 * PATCH), f32),
             pltpu.VMEM((PAIRS * 2 * BLOCKS, D), f32),
             pltpu.VMEM((PAIRS * 2 * BLOCKS, D), bf16),
-            pltpu.VMEM((2 * BLOCKS, 2 * PATCH), bf16),
+            pltpu.SemaphoreType.DMA,
         ],
         compiler_params=pltpu.CompilerParams(vmem_limit_bytes=ENCODE_VMEM),
         name="encode_frames",
     )(
-        tile, in_vmem(own), in_vmem(own_normed), in_vmem(other), gain, bias,
-        in_vmem(w_qkv), in_vmem(w_out), block_map,
+        in_vmem(own), in_vmem(own_normed), in_vmem(other), gain, bias,
+        in_vmem(w_qkv), in_hbm(w_out), in_vmem(pool),
     )
 
 
@@ -375,15 +402,15 @@
 def on_device(
     frames_in, norm_gain, norm_bias, w_qkv, w_out, time_taps, w_proj, clip_lengths, frame_slot, block_map
 ):
-    tile = lax.axis_index("tile")
-    sent = lax.dynamic_slice_in_dim(frames_in, FR_DEV * (1 - tile), FR_DEV)
+    core = jnp.reshape(lax.axis_index("tile"), (1,)).astype(jnp.int32)
+    sent = cut_sent(core, frames_in)
     other = lax.ppermute(sent, "tile", SWAP)
-    core = jnp.reshape(tile, (1,)).astype(jnp.int32)
-    core = jnp.reshape(tile, (1,)).astype(jnp.int32)
     frames_in, _ = lax.optimization_barrier((frames_in, sent))
-    own, own_normed, w_qkv, w_out = stage(core, frames_in, norm_gain, norm_bias, w_qkv, w_out)
+    own, own_normed, w_qkv, pool = stage(
+        core, frames_in, norm_gain, norm_bias, block_map[None], w_qkv
+    )
     pooled = encode(
-        core, own, own_normed, other, norm_gain, norm_bias, w_qkv, w_out, block_map[None]
+        own, own_normed, other, norm_gain, norm_bias, w_qkv, w_out, pool
     )
     spread = lax.all_to_all(pooled, "frame", split_axis=0, concat_axis=0, tiled=True)
     spread_other = lax.ppermute(spread, "tile", SWAP)

time: 89.3 us -> 87.3 us (0.978)
  local copies, waits for them, and re-layouts: 1.68 us -> 0.04 us
    dynamic_slice x1 -> x0, local copies, waits for them, and re-layouts: 1.64 us -> none  [on_device(): sent = lax.dynamic_slice_in_dim(frames_in, FR_DEV * (1 - tile), FR_DEV)]
    pallas_call x2 -> x3, Pallas kernels: 31.4 us -> 31.1 us  [the longest x1 25.7 us: encode(): pl.pallas_call(encode_kernel, in_specs=[vmem] * 6 + [hbm, vmem], out_spec...]
where the time goes in v3:
time: 87.3 us; the launch traced here: 87.2 us
  blocking collectives  44.2 us (51%)
  Pallas kernels  37.9 us (43%)
  starting transfers between devices  4.71 us (5%)
    all_to_all x1, blocking collectives, on_device(): lax.all_to_all(pooled, 'frame', split_axis=0, concat_axis=0, tiled=True)  27.6 us
    pallas_call x1, Pallas kernels, encode(): pl.pallas_call(encode_kernel, in_specs=[vmem] * 6 + [hbm, vmem], out_spec...  25.7 us
    all_to_all x1, blocking collectives, on_device(): lax.all_to_all(mixed, 'frame', split_axis=0, concat_axis=0, tiled=True)  16.6 us
    pallas_call x1, Pallas kernels, stage(): pl.pallas_call(stage_kernel, in_specs=[smem, hbm, vmem, vmem, vmem, hbm],...  3.89 us
    pallas_call x1, Pallas kernels, pick(): pl.pallas_call(pick_kernel, in_specs=[smem, smem, vmem, vmem], out_specs=...  2.16 us
    pallas_call x1, Pallas kernels, project(): pl.pallas_call(project_kernel, in_specs=[smem, vmem, vmem, vmem], out_spe...  1.97 us
  transfers between devices with their start and end apart: 3, of which 0 were waited for; matrix products, arithmetic and copies ran while one was open for 0% of the time, Pallas kernels for 9%

profile of v3, /device:TPU:1, one launch (start us, length us, event | category | flops | bytes accessed | tf_op | source)
XLA Modules:
  0.0 87.2 jit_solution(12663279093996274671)
XLA Ops:
  0.0 0.0 copy-start.2
  0.0 0.0 copy-start.1
  0.0 0.0 copy-start.5
  0.0 1.5 %cut_sent_half.1 = bf16[6,128,1152]{2,1,0:T(8,128)(2,1)S(1)} custom-call(s32[1]{0:T(128)} %bitcast.tile_ref, bf16[12,128,1152]{2,1,0:T(8,128)(2,1)} %frames_hbm.2), custom_call_target="tpu_custom_call" | custom-call | tf_op jit(solution)/shard_map/cut_sent_half/pallas_call | solution.py:72
  1.5 1.5 %collective-permute-start = (bf16[6,128,1152]{2,1,0:T(8,128)(2,1)S(1)}, bf16[6,128,1152]{2,1,0:T(8,128)(2,1)S(1)}, u32[]{:S(2)}, u32[]{:S(2)}) collective-permute-start(bf16[6,128,1152]{2,1,0:T(8,128)(2,1)S(1)} %cut_sent_half.1), channel_id=1, source_target_pairs={{0,1},{1,0},{2,3},{3,2},{4,5},{5,4},{6,7},{7,6},{8,9},{9,8},{10,11... | collective-permute-start | bytes 5308424 | tf_op jit(solution)/shard_map/ppermute | solution.py:407
  3.0 0.0 copy-done.2
  3.0 0.0 copy-done.1
  3.0 0.0 copy-done.5
  3.0 3.9 %stage_operands.1 = (bf16[6,128,1152]{2,1,0:T(8,128)(2,1)S(1)}, bf16[6,128,1152]{2,1,0:T(8,128)(2,1)S(1)}, bf16[1152,3456]{1,0:T(8,128)(2,1)S(1)}, bf16[128,512]{1,0:T(8,128)(2,1)S(1)}) custom-call(s32[1]{0:T(128)} %bitcast.tile_ref, bf16[12,128,1152]{2,1,0:T(8,128)(2,1)} %frames_hbm.2, f32[1152]{0:T(1024)S(1)} %copy-done.1, f32[1152]{0:T(1024)S(1)} %copy-done.2, ...), custom_call_target="tpu_custom_call" | custom-call | tf_op jit(solution)/shard_map/stage_operands/pallas_call | solution.py:105
  6.9 0.0 collective-permute-done.other_ref
  6.9 0.0 copy-start.6
  6.9 0.0 copy-start.4
  7.0 0.0 copy-start.3
  7.0 25.7 %encode_frames.1 = bf16[64,2,3456]{2,1,0:T(2,128)(2,1)S(1)} custom-call(bf16[6,128,1152]{2,1,0:T(8,128)(2,1)S(1)} %get-tuple-element.13.own_ref, bf16[6,128,1152]{2,1,0:T(8,128)(2,1)S(1)} %get-tuple-element.14.own_normed, bf16[6,128,1152]{2,1,0:T(8,128)(2,1)S(1)} %collective-permute-done.other_ref, f32[1152]{0:T(1024)S(1)} %copy-done.1, f32[1152]{0:T(1024)S(1)} %copy-done.2, ...), custom_call_target="tpu_custom_call" | custom-call | tf_op jit(solution)/shard_map/encode_frames/pallas_call | solution.py:217
  32.7 27.6 %all_to_all.10.own_ref = bf16[64,2,3456]{2,1,0:T(2,128)(2,1)S(1)} all-to-all(bf16[64,2,3456]{2,1,0:T(2,128)(2,1)S(1)} %encode_frames.1), channel_id=1, replica_groups=mesh['frame'=64,'tile'=2] {'frame'}, dimensions={0} | all-to-all | bytes 1769472 | tf_op jit(solution)/shard_map/all_to_all | solution.py:415
  60.3 1.6 %collective-permute-start.1 = (bf16[64,2,3456]{2,1,0:T(2,128)(2,1)S(1)}, bf16[64,2,3456]{2,1,0:T(2,128)(2,1)S(1)}, u32[]{:S(2)}, u32[]{:S(2)}) collective-permute-start(bf16[64,2,3456]{2,1,0:T(2,128)(2,1)S(1)} %all_to_all.10.own_ref), channel_id=1, source_target_pairs={{0,1},{1,0},{2,3},{3,2},{4,5},{5,4},{6,7},{7,6},{8,9},{9,8},{10,11... | collective-permute-start | bytes 2654216 | tf_op jit(solution)/shard_map/ppermute | solution.py:416
  61.8 0.0 copy-done.6
  61.8 0.0 copy-done.4
  61.8 2.2 %pick_own_rows.1 = (bf16[1152,384]{1,0:T(8,128)(2,1)S(1)}, f32[1152,640]{1,0:T(8,128)S(1)}) custom-call(s32[1]{0:T(128)} %bitcast.tile_ref, s32[6]{0:T(128)S(1)} %copy-done.4, s32[1,768]{1,0:T(1,128)S(1)} %broadcast_in_dim.7.slots_ref, bf16[64,2,3456]{2,1,0:T(2,128)(2,1)S(1)} %all_to_all.10.own_ref), custom_call_target="tpu_custom_call" | custom-call | tf_op jit(solution)/shard_map/pick_own_rows/pallas_call | solution.py:281
  64.0 0.0 collective-permute-done.1.other_ref
  64.0 0.0 copy-done.3
  64.0 0.0 copy-start
  64.0 1.2 %mix_rows.1 = bf16[64,2,1920]{2,1,0:T(2,128)(2,1)S(1)} custom-call(s32[1]{0:T(128)} %bitcast.tile_ref, bf16[64,2,3456]{2,1,0:T(2,128)(2,1)S(1)} %collective-permute-done.1.other_ref, bf16[1152,384]{1,0:T(8,128)(2,1)S(1)} %get-tuple-element.17.other_hit, f32[1152,640]{1,0:T(8,128)S(1)} %get-tuple-element.18.picked_ref, f32[3,1152]{1,0:T(4,128)S(1)} %copy-done.3), custom_call_target="tpu_custom_call" | custom-call | tf_op jit(solution)/shard_map/mix_rows/pallas_call | solution.py:315
  65.2 16.6 %all_to_all.11.own_ref = bf16[64,2,1920]{2,1,0:T(2,128)(2,1)S(1)} all-to-all(bf16[64,2,1920]{2,1,0:T(2,128)(2,1)S(1)} %mix_rows.1), channel_id=1, replica_groups=mesh['frame'=64,'tile'=2] {'frame'}, dimensions={0} | all-to-all | bytes 983040 | tf_op jit(solution)/shard_map/all_to_all | solution.py:419
  81.9 1.7 %collective-permute-start.2 = (bf16[64,2,1920]{2,1,0:T(2,128)(2,1)S(1)}, bf16[64,2,1920]{2,1,0:T(2,128)(2,1)S(1)}, u32[]{:S(2)}, u32[]{:S(2)}) collective-permute-start(bf16[64,2,1920]{2,1,0:T(2,128)(2,1)S(1)} %all_to_all.11.own_ref), channel_id=1, source_target_pairs={{0,1},{1,0},{2,3},{3,2},{4,5},{5,4},{6,7},{7,6},{8,9},{9,8},{10,11... | collective-permute-start | bytes 1474568 | tf_op jit(solution)/shard_map/ppermute | solution.py:420
  83.5 0.0 copy-done
  83.5 1.5 %project_own_channels.1.part_ref = f32[384,1792]{1,0:T(8,128)S(1)} custom-call(s32[1]{0:T(128)} %bitcast.tile_ref, bf16[64,2,1920]{2,1,0:T(2,128)(2,1)S(1)} %all_to_all.11.own_ref, bf16[1152,1792]{1,0:T(8,128)(2,1)S(1)} %copy-done), custom_call_target="tpu_custom_call" | custom-call | tf_op jit(solution)/shard_map/project_own_channels/pallas_call | solution.py:348
  85.0 0.0 collective-permute-done.2.other_ref
  85.0 2.0 %project_rows.1 = bf16[6,64,1792]{2,1,0:T(8,128)(2,1)} custom-call(s32[1]{0:T(128)} %bitcast.tile_ref, bf16[64,2,1920]{2,1,0:T(2,128)(2,1)S(1)} %collective-permute-done.2.other_ref, f32[384,1792]{1,0:T(8,128)S(1)} %project_own_channels.1.part_ref, bf16[1152,1792]{1,0:T(8,128)(2,1)S(1)} %copy-done), custom_call_target="tpu_custom_call" | custom-call | tf_op jit(solution)/shard_map/project_rows/pallas_call | solution.py:384
  (1 shorter events, 0.0 us)
Async XLA Ops:
  0.0 3.0 %copy-start.2 = (f32[1152]{0:T(1024)S(1)}, f32[1152]{0:T(1024)}, u32[]{:S(2)}) copy-start(f32[1152]{0:T(1024)} %bias_ref.3) | copy-start | bytes 13828
  0.0 3.0 %copy-start.1 = (f32[1152]{0:T(1024)S(1)}, f32[1152]{0:T(1024)}, u32[]{:S(2)}) copy-start(f32[1152]{0:T(1024)} %gain_ref.3) | copy-start | bytes 13828
  0.0 3.0 %copy-start.5 = (s32[64]{0:T(128)S(1)}, s32[64]{0:T(128)}, u32[]{:S(2)}) copy-start(s32[64]{0:T(128)} %param.19) | copy-start | bytes 772
  1.5 5.4 %collective-permute-start = (bf16[6,128,1152]{2,1,0:T(8,128)(2,1)S(1)}, bf16[6,128,1152]{2,1,0:T(8,128)(2,1)S(1)}, u32[]{:S(2)}, u32[]{:S(2)}) collective-permute-start(bf16[6,128,1152]{2,1,0:T(8,128)(2,1)S(1)} %cut_sent_half.1), channel_id=1, source_target_pairs={{0,1},{1,0},{2,3},{3,2},{4,5},{5,4},{6,7},{7,6},{8,9},{9,8},{10,11... | collective-permute-start | bytes 5308424 | tf_op jit(solution)/shard_map/ppermute | solution.py:407
  6.9 54.9 %copy-start.6 = (s32[768]{0:T(1024)S(1)}, s32[768]{0:T(1024)}, u32[]{:S(2)}) copy-start(s32[768]{0:T(1024)} %param.18) | copy-start | bytes 9220
  6.9 54.9 %copy-start.4 = (s32[6]{0:T(128)S(1)}, s32[6]{0:T(128)}, u32[]{:S(2)}) copy-start(s32[6]{0:T(128)} %lengths_ref.1) | copy-start | bytes 76
  7.0 57.1 %copy-start.3 = (f32[3,1152]{1,0:T(4,128)S(1)}, f32[3,1152]{1,0:T(4,128)}, u32[]{:S(2)}) copy-start(f32[3,1152]{1,0:T(4,128)} %taps_ref.1) | copy-start | bytes 41476
  60.3 3.7 %collective-permute-start.1 = (bf16[64,2,3456]{2,1,0:T(2,128)(2,1)S(1)}, bf16[64,2,3456]{2,1,0:T(2,128)(2,1)S(1)}, u32[]{:S(2)}, u32[]{:S(2)}) collective-permute-start(bf16[64,2,3456]{2,1,0:T(2,128)(2,1)S(1)} %all_to_all.10.own_ref), channel_id=1, source_target_pairs={{0,1},{1,0},{2,3},{3,2},{4,5},{5,4},{6,7},{7,6},{8,9},{9,8},{10,11... | collective-permute-start | bytes 2654216 | tf_op jit(solution)/shard_map/ppermute | solution.py:416
  64.0 19.5 %copy-start = (bf16[1152,1792]{1,0:T(8,128)(2,1)S(1)}, bf16[1152,1792]{1,0:T(8,128)(2,1)}, u32[]{:S(2)}) copy-start(bf16[1152,1792]{1,0:T(8,128)(2,1)} %w_ref.3) | copy-start | bytes 12386308
  81.9 3.1 %collective-permute-start.2 = (bf16[64,2,1920]{2,1,0:T(2,128)(2,1)S(1)}, bf16[64,2,1920]{2,1,0:T(2,128)(2,1)S(1)}, u32[]{:S(2)}, u32[]{:S(2)}) collective-permute-start(bf16[64,2,1920]{2,1,0:T(2,128)(2,1)S(1)} %all_to_all.11.own_ref), channel_id=1, source_target_pairs={{0,1},{1,0},{2,3},{3,2},{4,5},{5,4},{6,7},{7,6},{8,9},{9,8},{10,11... | collective-permute-start | bytes 1474568 | tf_op jit(solution)/shard_map/ppermute | solution.py:420

commit v4 on v3

--- a/solution.py
+++ b/solution.py
@@ -20,9 +20,10 @@
 SLOT_DEV = 12
 SLOTS = 768
 PAIRS = 3
+PIECES = 9
 PART = 640
 REST = 512
-OUT_CUT = 896
+OUT_CUTS = (0, 512, 1024, 1536, 1792)
 OUT_DEV = 1792
 NORM_EPS = 1e-6
 SCORE_SCALE = math.log2(math.e) / math.sqrt(HEAD_DIM)
@@ -86,8 +87,8 @@
 ):
     rows = pl.ds(FR_DEV * tile_ref[0], FR_DEV)
     copies = [pltpu.make_async_copy(frames_hbm.at[rows], own_ref, sems.at[0])]
-    step = D // 4
-    for n in range(4):
+    step = D // PIECES
+    for n in range(PIECES):
         part = pl.ds(n * step, step)
         copies.append(pltpu.make_async_copy(wqkv_hbm.at[part], wqkv_ref.at[part], sems.at[n + 1]))
     for copy in copies:
@@ -112,14 +113,15 @@
             pltpu.VMEM((D, 3 * D), bf16),
             pltpu.VMEM((2 * BLOCKS, 2 * PATCH), bf16),
         ],
-        scratch_shapes=[pltpu.SemaphoreType.DMA((5,))],
+        scratch_shapes=[pltpu.SemaphoreType.DMA((1 + PIECES,))],
         compiler_params=pltpu.CompilerParams(vmem_limit_bytes=STAGE_VMEM),
         name="stage_operands",
     )(tile, in_hbm(frames_in), gain, bias, block_map, in_hbm(w_qkv))
 
 
 def project_qkv(normed_s, w_ref, qk_s, vt_s):
-    for lo in range(0, 3 * D, 256):
+    starts = list(range(2 * D, 3 * D, 256)) + [0, 1024, 256, 1280, 512, 1536, 768, 1792, 2048]
+    for lo in starts:
         hi = min(lo + 256, 3 * D)
         part = jnp.dot(normed_s[...], w_ref[:, lo:hi], preferred_element_type=f32)
         if hi <= 2 * D:
@@ -363,13 +365,13 @@
         rows_s[j * 128 : (j + 1) * 128, :] = deinterleave(other_ref[:, :, cols].reshape(128, REST))
     first = pl.multiple_of(PART * (1 - tile), 128)
     copies = []
-    for n, lo in enumerate(range(0, OUT_DEV, OUT_CUT)):
-        for mid in range(lo, lo + OUT_CUT, 256):
-            cols = slice(mid, min(mid + 256, lo + OUT_CUT))
+    for n, (lo, hi) in enumerate(zip(OUT_CUTS[:-1], OUT_CUTS[1:])):
+        for mid in range(lo, hi, 256):
+            cols = slice(mid, mid + 256)
             weights = w_ref[pl.ds(first, REST), cols]
             out = jnp.dot(rows_s[...], weights, preferred_element_type=f32) + part_ref[:, cols]
-            out_s[:, :, cols] = out.astype(bf16).reshape(FR_DEV, BLOCKS, cols.stop - cols.start)
-        cols = pl.ds(lo, OUT_CUT)
+            out_s[:, :, cols] = out.astype(bf16).reshape(FR_DEV, BLOCKS, 256)
+        cols = pl.ds(lo, hi - lo)
         copies.append(
             pltpu.make_async_copy(out_s.at[:, :, cols], out_hbm.at[:, :, cols], sems.at[n])
         )
@@ -389,7 +391,7 @@
         scratch_shapes=[
             pltpu.VMEM((FR_DEV * BLOCKS, REST), bf16),
             pltpu.VMEM(shape, bf16),
-            pltpu.SemaphoreType.DMA((OUT_DEV // OUT_CUT,)),
+            pltpu.SemaphoreType.DMA((len(OUT_CUTS) - 1,)),
         ],
         compiler_params=pltpu.CompilerParams(vmem_limit_bytes=SMALL_VMEM),
         name="project_rows",

time: 87.3 us -> 86.9 us (level)
  no operation moved by 1% of the time
where the time goes in v4:
time: 86.9 us; the launch traced here: 86.8 us
  blocking collectives  44.2 us (51%)
  Pallas kernels  37.5 us (43%)
  starting transfers between devices  4.71 us (5%)
    all_to_all x1, blocking collectives, on_device(): lax.all_to_all(pooled, 'frame', split_axis=0, concat_axis=0, tiled=True)  27.6 us
    pallas_call x1, Pallas kernels, encode(): pl.pallas_call(encode_kernel, in_specs=[vmem] * 6 + [hbm, vmem], out_spec...  25.4 us
    all_to_all x1, blocking collectives, on_device(): lax.all_to_all(mixed, 'frame', split_axis=0, concat_axis=0, tiled=True)  16.6 us
    pallas_call x1, Pallas kernels, stage(): pl.pallas_call(stage_kernel, in_specs=[smem, hbm, vmem, vmem, vmem, hbm],...  3.86 us
    pallas_call x1, Pallas kernels, pick(): pl.pallas_call(pick_kernel, in_specs=[smem, smem, vmem, vmem], out_specs=...  2.16 us
    pallas_call x1, Pallas kernels, project(): pl.pallas_call(project_kernel, in_specs=[smem, vmem, vmem, vmem], out_spe...  1.9 us
  transfers between devices with their start and end apart: 3, of which 0 were waited for; matrix products, arithmetic and copies ran while one was open for 0% of the time, Pallas kernels for 9%

profile of v4, /device:TPU:1, one launch (start us, length us, event | category | flops | bytes accessed | tf_op | source)
XLA Modules:
  0.0 86.8 jit_solution(3605617561897393243)
XLA Ops:
  0.0 0.0 copy-start.2
  0.0 0.0 copy-start.1
  0.0 0.0 copy-start.5
  0.0 1.5 %cut_sent_half.1 = bf16[6,128,1152]{2,1,0:T(8,128)(2,1)S(1)} custom-call(s32[1]{0:T(128)} %bitcast.tile_ref, bf16[12,128,1152]{2,1,0:T(8,128)(2,1)} %frames_hbm.2), custom_call_target="tpu_custom_call" | custom-call | tf_op jit(solution)/shard_map/cut_sent_half/pallas_call | solution.py:73
  1.5 1.5 %collective-permute-start = (bf16[6,128,1152]{2,1,0:T(8,128)(2,1)S(1)}, bf16[6,128,1152]{2,1,0:T(8,128)(2,1)S(1)}, u32[]{:S(2)}, u32[]{:S(2)}) collective-permute-start(bf16[6,128,1152]{2,1,0:T(8,128)(2,1)S(1)} %cut_sent_half.1), channel_id=1, source_target_pairs={{0,1},{1,0},{2,3},{3,2},{4,5},{5,4},{6,7},{7,6},{8,9},{9,8},{10,11... | collective-permute-start | bytes 5308424 | tf_op jit(solution)/shard_map/ppermute | solution.py:409
  3.0 0.0 copy-done.2
  3.0 0.0 copy-done.1
  3.0 0.0 copy-done.5
  3.0 3.9 %stage_operands.1 = (bf16[6,128,1152]{2,1,0:T(8,128)(2,1)S(1)}, bf16[6,128,1152]{2,1,0:T(8,128)(2,1)S(1)}, bf16[1152,3456]{1,0:T(8,128)(2,1)S(1)}, bf16[128,512]{1,0:T(8,128)(2,1)S(1)}) custom-call(s32[1]{0:T(128)} %bitcast.tile_ref, bf16[12,128,1152]{2,1,0:T(8,128)(2,1)} %frames_hbm.2, f32[1152]{0:T(1024)S(1)} %copy-done.1, f32[1152]{0:T(1024)S(1)} %copy-done.2, ...), custom_call_target="tpu_custom_call" | custom-call | tf_op jit(solution)/shard_map/stage_operands/pallas_call | solution.py:106
  6.9 0.0 collective-permute-done.other_ref
  6.9 0.0 copy-start.6
  6.9 0.0 copy-start.4
  6.9 0.0 copy-start.3
  6.9 25.4 %encode_frames.1 = bf16[64,2,3456]{2,1,0:T(2,128)(2,1)S(1)} custom-call(bf16[6,128,1152]{2,1,0:T(8,128)(2,1)S(1)} %get-tuple-element.13.own_ref, bf16[6,128,1152]{2,1,0:T(8,128)(2,1)S(1)} %get-tuple-element.14.own_normed, bf16[6,128,1152]{2,1,0:T(8,128)(2,1)S(1)} %collective-permute-done.other_ref, f32[1152]{0:T(1024)S(1)} %copy-done.1, f32[1152]{0:T(1024)S(1)} %copy-done.2, ...), custom_call_target="tpu_custom_call" | custom-call | tf_op jit(solution)/shard_map/encode_frames/pallas_call | solution.py:219
  32.4 27.6 %all_to_all.10.own_ref = bf16[64,2,3456]{2,1,0:T(2,128)(2,1)S(1)} all-to-all(bf16[64,2,3456]{2,1,0:T(2,128)(2,1)S(1)} %encode_frames.1), channel_id=1, replica_groups=mesh['frame'=64,'tile'=2] {'frame'}, dimensions={0} | all-to-all | bytes 1769472 | tf_op jit(solution)/shard_map/all_to_all | solution.py:417
  59.9 1.6 %collective-permute-start.1 = (bf16[64,2,3456]{2,1,0:T(2,128)(2,1)S(1)}, bf16[64,2,3456]{2,1,0:T(2,128)(2,1)S(1)}, u32[]{:S(2)}, u32[]{:S(2)}) collective-permute-start(bf16[64,2,3456]{2,1,0:T(2,128)(2,1)S(1)} %all_to_all.10.own_ref), channel_id=1, source_target_pairs={{0,1},{1,0},{2,3},{3,2},{4,5},{5,4},{6,7},{7,6},{8,9},{9,8},{10,11... | collective-permute-start | bytes 2654216 | tf_op jit(solution)/shard_map/ppermute | solution.py:418
  61.5 0.0 copy-done.6
  61.5 0.0 copy-done.4
  61.5 2.2 %pick_own_rows.1 = (bf16[1152,384]{1,0:T(8,128)(2,1)S(1)}, f32[1152,640]{1,0:T(8,128)S(1)}) custom-call(s32[1]{0:T(128)} %bitcast.tile_ref, s32[6]{0:T(128)S(1)} %copy-done.4, s32[1,768]{1,0:T(1,128)S(1)} %broadcast_in_dim.7.slots_ref, bf16[64,2,3456]{2,1,0:T(2,128)(2,1)S(1)} %all_to_all.10.own_ref), custom_call_target="tpu_custom_call" | custom-call | tf_op jit(solution)/shard_map/pick_own_rows/pallas_call | solution.py:283
  63.7 0.0 collective-permute-done.1.other_ref
  63.7 0.0 copy-done.3
  63.7 0.0 copy-start
  63.7 1.2 %mix_rows.1 = bf16[64,2,1920]{2,1,0:T(2,128)(2,1)S(1)} custom-call(s32[1]{0:T(128)} %bitcast.tile_ref, bf16[64,2,3456]{2,1,0:T(2,128)(2,1)S(1)} %collective-permute-done.1.other_ref, bf16[1152,384]{1,0:T(8,128)(2,1)S(1)} %get-tuple-element.17.other_hit, f32[1152,640]{1,0:T(8,128)S(1)} %get-tuple-element.18.picked_ref, f32[3,1152]{1,0:T(4,128)S(1)} %copy-done.3), custom_call_target="tpu_custom_call" | custom-call | tf_op jit(solution)/shard_map/mix_rows/pallas_call | solution.py:317
  64.9 16.6 %all_to_all.11.own_ref = bf16[64,2,1920]{2,1,0:T(2,128)(2,1)S(1)} all-to-all(bf16[64,2,1920]{2,1,0:T(2,128)(2,1)S(1)} %mix_rows.1), channel_id=1, replica_groups=mesh['frame'=64,'tile'=2] {'frame'}, dimensions={0} | all-to-all | bytes 983040 | tf_op jit(solution)/shard_map/all_to_all | solution.py:421
  81.6 1.7 %collective-permute-start.2 = (bf16[64,2,1920]{2,1,0:T(2,128)(2,1)S(1)}, bf16[64,2,1920]{2,1,0:T(2,128)(2,1)S(1)}, u32[]{:S(2)}, u32[]{:S(2)}) collective-permute-start(bf16[64,2,1920]{2,1,0:T(2,128)(2,1)S(1)} %all_to_all.11.own_ref), channel_id=1, source_target_pairs={{0,1},{1,0},{2,3},{3,2},{4,5},{5,4},{6,7},{7,6},{8,9},{9,8},{10,11... | collective-permute-start | bytes 1474568 | tf_op jit(solution)/shard_map/ppermute | solution.py:422
  83.2 0.0 copy-done
  83.2 1.5 %project_own_channels.1.part_ref = f32[384,1792]{1,0:T(8,128)S(1)} custom-call(s32[1]{0:T(128)} %bitcast.tile_ref, bf16[64,2,1920]{2,1,0:T(2,128)(2,1)S(1)} %all_to_all.11.own_ref, bf16[1152,1792]{1,0:T(8,128)(2,1)S(1)} %copy-done), custom_call_target="tpu_custom_call" | custom-call | tf_op jit(solution)/shard_map/project_own_channels/pallas_call | solution.py:350
  84.7 0.0 collective-permute-done.2.other_ref
  84.7 1.9 %project_rows.1 = bf16[6,64,1792]{2,1,0:T(8,128)(2,1)} custom-call(s32[1]{0:T(128)} %bitcast.tile_ref, bf16[64,2,1920]{2,1,0:T(2,128)(2,1)S(1)} %collective-permute-done.2.other_ref, f32[384,1792]{1,0:T(8,128)S(1)} %project_own_channels.1.part_ref, bf16[1152,1792]{1,0:T(8,128)(2,1)S(1)} %copy-done), custom_call_target="tpu_custom_call" | custom-call | tf_op jit(solution)/shard_map/project_rows/pallas_call | solution.py:386
  (1 shorter events, 0.0 us)
Async XLA Ops:
  0.0 3.0 %copy-start.2 = (f32[1152]{0:T(1024)S(1)}, f32[1152]{0:T(1024)}, u32[]{:S(2)}) copy-start(f32[1152]{0:T(1024)} %bias_ref.3) | copy-start | bytes 13828
  0.0 3.0 %copy-start.1 = (f32[1152]{0:T(1024)S(1)}, f32[1152]{0:T(1024)}, u32[]{:S(2)}) copy-start(f32[1152]{0:T(1024)} %gain_ref.3) | copy-start | bytes 13828
  0.0 3.0 %copy-start.5 = (s32[64]{0:T(128)S(1)}, s32[64]{0:T(128)}, u32[]{:S(2)}) copy-start(s32[64]{0:T(128)} %param.19) | copy-start | bytes 772
  1.5 5.4 %collective-permute-start = (bf16[6,128,1152]{2,1,0:T(8,128)(2,1)S(1)}, bf16[6,128,1152]{2,1,0:T(8,128)(2,1)S(1)}, u32[]{:S(2)}, u32[]{:S(2)}) collective-permute-start(bf16[6,128,1152]{2,1,0:T(8,128)(2,1)S(1)} %cut_sent_half.1), channel_id=1, source_target_pairs={{0,1},{1,0},{2,3},{3,2},{4,5},{5,4},{6,7},{7,6},{8,9},{9,8},{10,11... | collective-permute-start | bytes 5308424 | tf_op jit(solution)/shard_map/ppermute | solution.py:409
  6.9 54.6 %copy-start.6 = (s32[768]{0:T(1024)S(1)}, s32[768]{0:T(1024)}, u32[]{:S(2)}) copy-start(s32[768]{0:T(1024)} %param.18) | copy-start | bytes 9220
  6.9 54.6 %copy-start.4 = (s32[6]{0:T(128)S(1)}, s32[6]{0:T(128)}, u32[]{:S(2)}) copy-start(s32[6]{0:T(128)} %lengths_ref.1) | copy-start | bytes 76
  6.9 56.8 %copy-start.3 = (f32[3,1152]{1,0:T(4,128)S(1)}, f32[3,1152]{1,0:T(4,128)}, u32[]{:S(2)}) copy-start(f32[3,1152]{1,0:T(4,128)} %taps_ref.1) | copy-start | bytes 41476
  59.9 3.7 %collective-permute-start.1 = (bf16[64,2,3456]{2,1,0:T(2,128)(2,1)S(1)}, bf16[64,2,3456]{2,1,0:T(2,128)(2,1)S(1)}, u32[]{:S(2)}, u32[]{:S(2)}) collective-permute-start(bf16[64,2,3456]{2,1,0:T(2,128)(2,1)S(1)} %all_to_all.10.own_ref), channel_id=1, source_target_pairs={{0,1},{1,0},{2,3},{3,2},{4,5},{5,4},{6,7},{7,6},{8,9},{9,8},{10,11... | collective-permute-start | bytes 2654216 | tf_op jit(solution)/shard_map/ppermute | solution.py:418
  63.7 19.5 %copy-start = (bf16[1152,1792]{1,0:T(8,128)(2,1)S(1)}, bf16[1152,1792]{1,0:T(8,128)(2,1)}, u32[]{:S(2)}) copy-start(bf16[1152,1792]{1,0:T(8,128)(2,1)} %w_ref.3) | copy-start | bytes 12386308
  81.6 3.1 %collective-permute-start.2 = (bf16[64,2,1920]{2,1,0:T(2,128)(2,1)S(1)}, bf16[64,2,1920]{2,1,0:T(2,128)(2,1)S(1)}, u32[]{:S(2)}, u32[]{:S(2)}) collective-permute-start(bf16[64,2,1920]{2,1,0:T(2,128)(2,1)S(1)} %all_to_all.11.own_ref), channel_id=1, source_target_pairs={{0,1},{1,0},{2,3},{3,2},{4,5},{5,4},{6,7},{7,6},{8,9},{9,8},{10,11... | collective-permute-start | bytes 1474568 | tf_op jit(solution)/shard_map/ppermute | solution.py:422

commit v5 on v4

--- a/solution.py
+++ b/solution.py
@@ -160,10 +160,10 @@
     items = [(s, head) for s in range(2) for head in range(HEADS)]
     score, weights = {}, {}
     for n in range(-6, len(items)):
-        if n + 6 < len(items):
-            score[n + 6] = scores(*items[n + 6])
         if 0 <= n + 3 < len(items):
             weights[n + 3] = weigh(score.pop(n + 3))
+        if 0 <= n + 6 < len(items):
+            score[n + 6] = scores(*items[n + 6])
         if n >= 0:
             total(*items[n], weights.pop(n))
 
@@ -245,8 +245,17 @@
         rows_s[j * 128 : (j + 1) * 128, :] = ref[:, :, cols].reshape(128, PART)
 
 
+def tap_sum(picked, taps, step):
+    total = 0.0
+    for tap in range(3):
+        first = (PAIRS * step + tap) * 128
+        total += taps[tap : tap + 1] * picked[first : first + 128, :]
+    return total
+
+
 def pick_kernel(
-    tile_ref, lengths_ref, slots_ref, own_ref, other_hit, picked_ref, rows_s, own_hit
+    tile_ref, lengths_ref, slots_ref, own_ref, taps_ref, other_hit, mixed_ref,
+    rows_s, own_hit, picked_s,
 ):
     tile = tile_ref[0]
     own_rows(own_ref, rows_s, tile)
@@ -275,44 +284,44 @@
             hit = jnp.where(held == want, 1.0, 0.0).astype(bf16)
             own_hit[rows, :] = hit[:, : SLOTS // 2]
             other_hit[rows, :] = hit[:, SLOTS // 2 :]
-    picked_ref[...] = jnp.dot(own_hit[...], rows_s[...], preferred_element_type=f32)
-
-
-def pick(tile, lengths, slots, own):
+    picked_s[...] = jnp.dot(own_hit[...], rows_s[...], preferred_element_type=f32)
+    taps = taps_ref[:, pl.ds(pl.multiple_of(512 * tile, 128), PART)]
+    for step in range(PAIRS):
+        mixed_ref[step * 128 : (step + 1) * 128, :] = tap_sum(picked_s, taps, step)
+
+
+def pick(tile, lengths, slots, own, taps):
     smem, vmem = (pl.BlockSpec(memory_space=m) for m in (pltpu.SMEM, pltpu.VMEM))
     return pl.pallas_call(
         pick_kernel,
-        in_specs=[smem, smem, vmem, vmem],
+        in_specs=[smem, smem, vmem, vmem, vmem],
         out_specs=[vmem, vmem],
         out_shape=[
             pltpu.VMEM((9 * 128, SLOTS // 2), bf16),
-            pltpu.VMEM((9 * 128, PART), f32),
+            pltpu.VMEM((PAIRS * 128, PART), f32),
         ],
         scratch_shapes=[
             pltpu.VMEM((SLOTS // 2, PART), bf16),
             pltpu.VMEM((9 * 128, SLOTS // 2), bf16),
+            pltpu.VMEM((9 * 128, PART), f32),
         ],
         compiler_params=pltpu.CompilerParams(vmem_limit_bytes=SMALL_VMEM),
         name="pick_own_rows",
-    )(tile, lengths, slots, in_vmem(own))
-
-
-def mix_kernel(tile_ref, other_ref, other_hit, picked_ref, taps_ref, out_ref, rows_s, picked_s):
+    )(tile, lengths, slots, in_vmem(own), taps)
+
+
+def mix_kernel(tile_ref, other_ref, other_hit, own_mixed, taps_ref, out_ref, rows_s, picked_s):
     tile = tile_ref[0]
     own_rows(other_ref, rows_s, tile)
     picked_s[...] = jnp.dot(other_hit[...], rows_s[...], preferred_element_type=f32)
     taps = taps_ref[:, pl.ds(pl.multiple_of(512 * tile, 128), PART)]
     for step in range(PAIRS):
-        mixed = 0.0
-        for tap in range(3):
-            first = (PAIRS * step + tap) * 128
-            rows = slice(first, first + 128)
-            mixed += taps[tap : tap + 1] * (picked_s[rows, :] + picked_ref[rows, :])
+        mixed = own_mixed[step * 128 : (step + 1) * 128, :] + tap_sum(picked_s, taps, step)
         mixed = mixed.astype(bf16).reshape(FRAME_DEVS, 2, PART)
         out_ref[:, :, step * PART : (step + 1) * PART] = mixed
 
 
-def mix(tile, other, other_hit, picked, taps):
+def mix(tile, other, other_hit, own_mixed, taps):
     smem, vmem = (pl.BlockSpec(memory_space=m) for m in (pltpu.SMEM, pltpu.VMEM))
     return pl.pallas_call(
         mix_kernel,
@@ -325,7 +334,7 @@
         ],
         compiler_params=pltpu.CompilerParams(vmem_limit_bytes=SMALL_VMEM),
         name="mix_rows",
-    )(tile, in_vmem(other), in_vmem(other_hit), in_vmem(picked), taps)
+    )(tile, in_vmem(other), in_vmem(other_hit), in_vmem(own_mixed), taps)
 
 
 def deinterleave(rows):
@@ -416,8 +425,8 @@
     )
     spread = lax.all_to_all(pooled, "frame", split_axis=0, concat_axis=0, tiled=True)
     spread_other = lax.ppermute(spread, "tile", SWAP)
-    other_hit, picked = pick(core, clip_lengths, frame_slot[None], spread)
-    mixed = mix(core, spread_other, other_hit, picked, time_taps)
+    other_hit, own_mixed = pick(core, clip_lengths, frame_slot[None], spread, time_taps)
+    mixed = mix(core, spread_other, other_hit, own_mixed, time_taps)
     home = lax.all_to_all(mixed, "frame", split_axis=0, concat_axis=0, tiled=True)
     home_other = lax.ppermute(home, "tile", SWAP)
     part = project_own(core, home, w_proj)

time: 86.9 us -> 86.7 us (level)
  no operation moved by 1% of the time
where the time goes in v5:
time: 86.7 us; the launch traced here: 86.5 us
  blocking collectives  44.1 us (51%)
  Pallas kernels  37.4 us (43%)
  starting transfers between devices  4.71 us (5%)
    all_to_all x1, blocking collectives, on_device(): lax.all_to_all(pooled, 'frame', split_axis=0, concat_axis=0, tiled=True)  27.6 us
    pallas_call x1, Pallas kernels, encode(): pl.pallas_call(encode_kernel, in_specs=[vmem] * 6 + [hbm, vmem], out_spec...  25.4 us
    all_to_all x1, blocking collectives, on_device(): lax.all_to_all(mixed, 'frame', split_axis=0, concat_axis=0, tiled=True)  16.5 us
    pallas_call x1, Pallas kernels, stage(): pl.pallas_call(stage_kernel, in_specs=[smem, hbm, vmem, vmem, vmem, hbm],...  3.86 us
    pallas_call x1, Pallas kernels, pick(): pl.pallas_call(pick_kernel, in_specs=[smem, smem, vmem, vmem, vmem], out_...  2.19 us
    pallas_call x1, Pallas kernels, project(): pl.pallas_call(project_kernel, in_specs=[smem, vmem, vmem, vmem], out_spe...  1.9 us
  transfers between devices with their start and end apart: 3, of which 0 were waited for; matrix products, arithmetic and copies ran while one was open for 0% of the time, Pallas kernels for 9%

profile of v5, /device:TPU:1, one launch (start us, length us, event | category | flops | bytes accessed | tf_op | source)
XLA Modules:
  0.0 86.5 jit_solution(1761059567396019697)
XLA Ops:
  0.0 0.0 copy-start.2
  0.0 0.0 copy-start.3
  0.0 0.0 copy-start.5
  0.0 1.5 %cut_sent_half.1 = bf16[6,128,1152]{2,1,0:T(8,128)(2,1)S(1)} custom-call(s32[1]{0:T(128)} %bitcast.tile_ref, bf16[12,128,1152]{2,1,0:T(8,128)(2,1)} %frames_hbm.2), custom_call_target="tpu_custom_call" | custom-call | tf_op jit(solution)/shard_map/cut_sent_half/pallas_call | solution.py:73
  1.5 1.5 %collective-permute-start = (bf16[6,128,1152]{2,1,0:T(8,128)(2,1)S(1)}, bf16[6,128,1152]{2,1,0:T(8,128)(2,1)S(1)}, u32[]{:S(2)}, u32[]{:S(2)}) collective-permute-start(bf16[6,128,1152]{2,1,0:T(8,128)(2,1)S(1)} %cut_sent_half.1), channel_id=1, source_target_pairs={{0,1},{1,0},{2,3},{3,2},{4,5},{5,4},{6,7},{7,6},{8,9},{9,8},{10,11... | collective-permute-start | bytes 5308424 | tf_op jit(solution)/shard_map/ppermute | solution.py:418
  3.0 0.0 copy-done.2
  3.0 0.0 copy-done.3
  3.0 0.0 copy-done.5
  3.0 3.9 %stage_operands.1 = (bf16[6,128,1152]{2,1,0:T(8,128)(2,1)S(1)}, bf16[6,128,1152]{2,1,0:T(8,128)(2,1)S(1)}, bf16[1152,3456]{1,0:T(8,128)(2,1)S(1)}, bf16[128,512]{1,0:T(8,128)(2,1)S(1)}) custom-call(s32[1]{0:T(128)} %bitcast.tile_ref, bf16[12,128,1152]{2,1,0:T(8,128)(2,1)} %frames_hbm.2, f32[1152]{0:T(1024)S(1)} %copy-done.2, f32[1152]{0:T(1024)S(1)} %copy-done.3, ...), custom_call_target="tpu_custom_call" | custom-call | tf_op jit(solution)/shard_map/stage_operands/pallas_call | solution.py:106
  6.9 0.0 collective-permute-done.other_ref
  6.9 0.0 copy-start.6
  6.9 0.0 copy-start.1
  6.9 0.0 copy-start.4
  6.9 25.4 %encode_frames.1 = bf16[64,2,3456]{2,1,0:T(2,128)(2,1)S(1)} custom-call(bf16[6,128,1152]{2,1,0:T(8,128)(2,1)S(1)} %get-tuple-element.13.own_ref, bf16[6,128,1152]{2,1,0:T(8,128)(2,1)S(1)} %get-tuple-element.14.own_normed, bf16[6,128,1152]{2,1,0:T(8,128)(2,1)S(1)} %collective-permute-done.other_ref, f32[1152]{0:T(1024)S(1)} %copy-done.2, f32[1152]{0:T(1024)S(1)} %copy-done.3, ...), custom_call_target="tpu_custom_call" | custom-call | tf_op jit(solution)/shard_map/encode_frames/pallas_call | solution.py:219
  32.4 27.6 %all_to_all.10.own_ref = bf16[64,2,3456]{2,1,0:T(2,128)(2,1)S(1)} all-to-all(bf16[64,2,3456]{2,1,0:T(2,128)(2,1)S(1)} %encode_frames.1), channel_id=1, replica_groups=mesh['frame'=64,'tile'=2] {'frame'}, dimensions={0} | all-to-all | bytes 1769472 | tf_op jit(solution)/shard_map/all_to_all | solution.py:426
  59.9 0.0 copy-start
  59.9 1.6 %collective-permute-start.1 = (bf16[64,2,3456]{2,1,0:T(2,128)(2,1)S(1)}, bf16[64,2,3456]{2,1,0:T(2,128)(2,1)S(1)}, u32[]{:S(2)}, u32[]{:S(2)}) collective-permute-start(bf16[64,2,3456]{2,1,0:T(2,128)(2,1)S(1)} %all_to_all.10.own_ref), channel_id=1, source_target_pairs={{0,1},{1,0},{2,3},{3,2},{4,5},{5,4},{6,7},{7,6},{8,9},{9,8},{10,11... | collective-permute-start | bytes 2654216 | tf_op jit(solution)/shard_map/ppermute | solution.py:427
  61.5 0.0 copy-done.6
  61.5 0.0 copy-done.1
  61.5 0.0 copy-done.4
  61.5 2.2 %pick_own_rows.1 = (bf16[1152,384]{1,0:T(8,128)(2,1)S(1)}, f32[384,640]{1,0:T(8,128)S(1)}) custom-call(s32[1]{0:T(128)} %bitcast.tile_ref, s32[6]{0:T(128)S(1)} %copy-done.4, s32[1,768]{1,0:T(1,128)S(1)} %broadcast_in_dim.7.slots_ref, bf16[64,2,3456]{2,1,0:T(2,128)(2,1)S(1)} %all_to_all.10.own_ref, f32[3,1152]{1,0:T(4,128)S(1)} %copy-done.1), custom_call_target="tpu_custom_call" | custom-call | tf_op jit(solution)/shard_map/pick_own_rows/pallas_call | solution.py:295
  63.7 0.0 collective-permute-done.1.other_ref
  63.7 1.1 %mix_rows.1 = bf16[64,2,1920]{2,1,0:T(2,128)(2,1)S(1)} custom-call(s32[1]{0:T(128)} %bitcast.tile_ref, bf16[64,2,3456]{2,1,0:T(2,128)(2,1)S(1)} %collective-permute-done.1.other_ref, bf16[1152,384]{1,0:T(8,128)(2,1)S(1)} %get-tuple-element.17.other_hit, f32[384,640]{1,0:T(8,128)S(1)} %get-tuple-element.18.own_mixed, f32[3,1152]{1,0:T(4,128)S(1)} %copy-done.1), custom_call_target="tpu_custom_call" | custom-call | tf_op jit(solution)/shard_map/mix_rows/pallas_call | solution.py:326
  64.8 16.5 %all_to_all.11.own_ref = bf16[64,2,1920]{2,1,0:T(2,128)(2,1)S(1)} all-to-all(bf16[64,2,1920]{2,1,0:T(2,128)(2,1)S(1)} %mix_rows.1), channel_id=1, replica_groups=mesh['frame'=64,'tile'=2] {'frame'}, dimensions={0} | all-to-all | bytes 983040 | tf_op jit(solution)/shard_map/all_to_all | solution.py:430
  81.3 1.7 %collective-permute-start.2 = (bf16[64,2,1920]{2,1,0:T(2,128)(2,1)S(1)}, bf16[64,2,1920]{2,1,0:T(2,128)(2,1)S(1)}, u32[]{:S(2)}, u32[]{:S(2)}) collective-permute-start(bf16[64,2,1920]{2,1,0:T(2,128)(2,1)S(1)} %all_to_all.11.own_ref), channel_id=1, source_target_pairs={{0,1},{1,0},{2,3},{3,2},{4,5},{5,4},{6,7},{7,6},{8,9},{9,8},{10,11... | collective-permute-start | bytes 1474568 | tf_op jit(solution)/shard_map/ppermute | solution.py:431
  83.0 0.0 copy-done
  83.0 1.5 %project_own_channels.1.part_ref = f32[384,1792]{1,0:T(8,128)S(1)} custom-call(s32[1]{0:T(128)} %bitcast.tile_ref, bf16[64,2,1920]{2,1,0:T(2,128)(2,1)S(1)} %all_to_all.11.own_ref, bf16[1152,1792]{1,0:T(8,128)(2,1)S(1)} %copy-done), custom_call_target="tpu_custom_call" | custom-call | tf_op jit(solution)/shard_map/project_own_channels/pallas_call | solution.py:359
  84.4 0.0 collective-permute-done.2.other_ref
  84.5 1.9 %project_rows.1 = bf16[6,64,1792]{2,1,0:T(8,128)(2,1)} custom-call(s32[1]{0:T(128)} %bitcast.tile_ref, bf16[64,2,1920]{2,1,0:T(2,128)(2,1)S(1)} %collective-permute-done.2.other_ref, f32[384,1792]{1,0:T(8,128)S(1)} %project_own_channels.1.part_ref, bf16[1152,1792]{1,0:T(8,128)(2,1)S(1)} %copy-done), custom_call_target="tpu_custom_call" | custom-call | tf_op jit(solution)/shard_map/project_rows/pallas_call | solution.py:395
  (1 shorter events, 0.0 us)
Async XLA Ops:
  0.0 3.0 %copy-start.2 = (f32[1152]{0:T(1024)S(1)}, f32[1152]{0:T(1024)}, u32[]{:S(2)}) copy-start(f32[1152]{0:T(1024)} %gain_ref.3) | copy-start | bytes 13828
  0.0 3.0 %copy-start.3 = (f32[1152]{0:T(1024)S(1)}, f32[1152]{0:T(1024)}, u32[]{:S(2)}) copy-start(f32[1152]{0:T(1024)} %bias_ref.3) | copy-start | bytes 13828
  0.0 3.0 %copy-start.5 = (s32[64]{0:T(128)S(1)}, s32[64]{0:T(128)}, u32[]{:S(2)}) copy-start(s32[64]{0:T(128)} %param.19) | copy-start | bytes 772
  1.5 5.4 %collective-permute-start = (bf16[6,128,1152]{2,1,0:T(8,128)(2,1)S(1)}, bf16[6,128,1152]{2,1,0:T(8,128)(2,1)S(1)}, u32[]{:S(2)}, u32[]{:S(2)}) collective-permute-start(bf16[6,128,1152]{2,1,0:T(8,128)(2,1)S(1)} %cut_sent_half.1), channel_id=1, source_target_pairs={{0,1},{1,0},{2,3},{3,2},{4,5},{5,4},{6,7},{7,6},{8,9},{9,8},{10,11... | collective-permute-start | bytes 5308424 | tf_op jit(solution)/shard_map/ppermute | solution.py:418
  6.9 54.6 %copy-start.6 = (s32[768]{0:T(1024)S(1)}, s32[768]{0:T(1024)}, u32[]{:S(2)}) copy-start(s32[768]{0:T(1024)} %param.18) | copy-start | bytes 9220
  6.9 54.6 %copy-start.1 = (f32[3,1152]{1,0:T(4,128)S(1)}, f32[3,1152]{1,0:T(4,128)}, u32[]{:S(2)}) copy-start(f32[3,1152]{1,0:T(4,128)} %taps_ref.3) | copy-start | bytes 41476
  6.9 54.6 %copy-start.4 = (s32[6]{0:T(128)S(1)}, s32[6]{0:T(128)}, u32[]{:S(2)}) copy-start(s32[6]{0:T(128)} %lengths_ref.1) | copy-start | bytes 76
  59.9 23.1 %copy-start = (bf16[1152,1792]{1,0:T(8,128)(2,1)S(1)}, bf16[1152,1792]{1,0:T(8,128)(2,1)}, u32[]{:S(2)}) copy-start(bf16[1152,1792]{1,0:T(8,128)(2,1)} %w_ref.3) | copy-start | bytes 12386308
  59.9 3.8 %collective-permute-start.1 = (bf16[64,2,3456]{2,1,0:T(2,128)(2,1)S(1)}, bf16[64,2,3456]{2,1,0:T(2,128)(2,1)S(1)}, u32[]{:S(2)}, u32[]{:S(2)}) collective-permute-start(bf16[64,2,3456]{2,1,0:T(2,128)(2,1)S(1)} %all_to_all.10.own_ref), channel_id=1, source_target_pairs={{0,1},{1,0},{2,3},{3,2},{4,5},{5,4},{6,7},{7,6},{8,9},{9,8},{10,11... | collective-permute-start | bytes 2654216 | tf_op jit(solution)/shard_map/ppermute | solution.py:427
  81.3 3.1 %collective-permute-start.2 = (bf16[64,2,1920]{2,1,0:T(2,128)(2,1)S(1)}, bf16[64,2,1920]{2,1,0:T(2,128)(2,1)S(1)}, u32[]{:S(2)}, u32[]{:S(2)}) collective-permute-start(bf16[64,2,1920]{2,1,0:T(2,128)(2,1)S(1)} %all_to_all.11.own_ref), channel_id=1, source_target_pairs={{0,1},{1,0},{2,3},{3,2},{4,5},{5,4},{6,7},{7,6},{8,9},{9,8},{10,11... | collective-permute-start | bytes 1474568 | tf_op jit(solution)/shard_map/ppermute | solution.py:431

commit v6 on v5

--- a/solution.py
+++ b/solution.py
@@ -60,11 +60,12 @@
 def cut_kernel(tile_ref, frames_hbm, out_ref, sems):
     first = FR_DEV * (1 - tile_ref[0])
     copies = []
-    for f in range(FR_DEV):
+    for n in range(2):
+        source = frames_hbm.at[pl.ds(first + PAIRS * n, PAIRS)]
         copies.append(
-            pltpu.make_async_copy(frames_hbm.at[first + f], out_ref.at[f], sems.at[f])
+            pltpu.make_async_copy(source, out_ref.at[pl.ds(PAIRS * n, PAIRS)], sems.at[n])
         )
-        copies[f].start()
+        copies[n].start()
     for copy in copies:
         copy.wait()
 
@@ -75,7 +76,7 @@
         in_specs=[pl.BlockSpec(memory_space=m) for m in (pltpu.SMEM, pltpu.HBM)],
         out_specs=pl.BlockSpec(memory_space=pltpu.VMEM),
         out_shape=pltpu.VMEM((FR_DEV, HALF, D), bf16),
-        scratch_shapes=[pltpu.SemaphoreType.DMA((FR_DEV,))],
+        scratch_shapes=[pltpu.SemaphoreType.DMA((2,))],
         compiler_params=pltpu.CompilerParams(vmem_limit_bytes=STAGE_VMEM),
         name="cut_sent_half",
     )(tile, in_hbm(frames_in))

time: 86.7 us -> 86.7 us (level)
  no operation moved by 1% of the time
where the time goes in v6:
time: 86.7 us; the launch traced here: 86.5 us
  blocking collectives  44.1 us (51%)
  Pallas kernels  37.4 us (43%)
  starting transfers between devices  4.71 us (5%)
    all_to_all x1, blocking collectives, on_device(): lax.all_to_all(pooled, 'frame', split_axis=0, concat_axis=0, tiled=True)  27.6 us
    pallas_call x1, Pallas kernels, encode(): pl.pallas_call(encode_kernel, in_specs=[vmem] * 6 + [hbm, vmem], out_spec...  25.4 us
    all_to_all x1, blocking collectives, on_device(): lax.all_to_all(mixed, 'frame', split_axis=0, concat_axis=0, tiled=True)  16.5 us
    pallas_call x1, Pallas kernels, stage(): pl.pallas_call(stage_kernel, in_specs=[smem, hbm, vmem, vmem, vmem, hbm],...  3.86 us
    pallas_call x1, Pallas kernels, pick(): pl.pallas_call(pick_kernel, in_specs=[smem, smem, vmem, vmem, vmem], out_...  2.19 us
    pallas_call x1, Pallas kernels, project(): pl.pallas_call(project_kernel, in_specs=[smem, vmem, vmem, vmem], out_spe...  1.9 us
  transfers between devices with their start and end apart: 3, of which 0 were waited for; matrix products, arithmetic and copies ran while one was open for 0% of the time, Pallas kernels for 9%

profile of v6, /device:TPU:1, one launch (start us, length us, event | category | flops | bytes accessed | tf_op | source)
XLA Modules:
  0.0 86.5 jit_solution(8782778203160789323)
XLA Ops:
  0.0 0.0 copy-start.2
  0.0 0.0 copy-start.3
  0.0 0.0 copy-start.5
  0.0 1.5 %cut_sent_half.1 = bf16[6,128,1152]{2,1,0:T(8,128)(2,1)S(1)} custom-call(s32[1]{0:T(128)} %bitcast.tile_ref, bf16[12,128,1152]{2,1,0:T(8,128)(2,1)} %frames_hbm.2), custom_call_target="tpu_custom_call" | custom-call | tf_op jit(solution)/shard_map/cut_sent_half/pallas_call | solution.py:74
  1.5 1.5 %collective-permute-start = (bf16[6,128,1152]{2,1,0:T(8,128)(2,1)S(1)}, bf16[6,128,1152]{2,1,0:T(8,128)(2,1)S(1)}, u32[]{:S(2)}, u32[]{:S(2)}) collective-permute-start(bf16[6,128,1152]{2,1,0:T(8,128)(2,1)S(1)} %cut_sent_half.1), channel_id=1, source_target_pairs={{0,1},{1,0},{2,3},{3,2},{4,5},{5,4},{6,7},{7,6},{8,9},{9,8},{10,11... | collective-permute-start | bytes 5308424 | tf_op jit(solution)/shard_map/ppermute | solution.py:419
  3.0 0.0 copy-done.2
  3.0 0.0 copy-done.3
  3.0 0.0 copy-done.5
  3.0 3.9 %stage_operands.1 = (bf16[6,128,1152]{2,1,0:T(8,128)(2,1)S(1)}, bf16[6,128,1152]{2,1,0:T(8,128)(2,1)S(1)}, bf16[1152,3456]{1,0:T(8,128)(2,1)S(1)}, bf16[128,512]{1,0:T(8,128)(2,1)S(1)}) custom-call(s32[1]{0:T(128)} %bitcast.tile_ref, bf16[12,128,1152]{2,1,0:T(8,128)(2,1)} %frames_hbm.2, f32[1152]{0:T(1024)S(1)} %copy-done.2, f32[1152]{0:T(1024)S(1)} %copy-done.3, ...), custom_call_target="tpu_custom_call" | custom-call | tf_op jit(solution)/shard_map/stage_operands/pallas_call | solution.py:107
  6.9 0.0 collective-permute-done.other_ref
  6.9 0.0 copy-start.6
  6.9 0.0 copy-start.1
  6.9 0.0 copy-start.4
  6.9 25.4 %encode_frames.1 = bf16[64,2,3456]{2,1,0:T(2,128)(2,1)S(1)} custom-call(bf16[6,128,1152]{2,1,0:T(8,128)(2,1)S(1)} %get-tuple-element.13.own_ref, bf16[6,128,1152]{2,1,0:T(8,128)(2,1)S(1)} %get-tuple-element.14.own_normed, bf16[6,128,1152]{2,1,0:T(8,128)(2,1)S(1)} %collective-permute-done.other_ref, f32[1152]{0:T(1024)S(1)} %copy-done.2, f32[1152]{0:T(1024)S(1)} %copy-done.3, ...), custom_call_target="tpu_custom_call" | custom-call | tf_op jit(solution)/shard_map/encode_frames/pallas_call | solution.py:220
  32.3 27.6 %all_to_all.10.own_ref = bf16[64,2,3456]{2,1,0:T(2,128)(2,1)S(1)} all-to-all(bf16[64,2,3456]{2,1,0:T(2,128)(2,1)S(1)} %encode_frames.1), channel_id=1, replica_groups=mesh['frame'=64,'tile'=2] {'frame'}, dimensions={0} | all-to-all | bytes 1769472 | tf_op jit(solution)/shard_map/all_to_all | solution.py:427
  59.9 0.0 copy-start
  59.9 1.6 %collective-permute-start.1 = (bf16[64,2,3456]{2,1,0:T(2,128)(2,1)S(1)}, bf16[64,2,3456]{2,1,0:T(2,128)(2,1)S(1)}, u32[]{:S(2)}, u32[]{:S(2)}) collective-permute-start(bf16[64,2,3456]{2,1,0:T(2,128)(2,1)S(1)} %all_to_all.10.own_ref), channel_id=1, source_target_pairs={{0,1},{1,0},{2,3},{3,2},{4,5},{5,4},{6,7},{7,6},{8,9},{9,8},{10,11... | collective-permute-start | bytes 2654216 | tf_op jit(solution)/shard_map/ppermute | solution.py:428
  61.5 0.0 copy-done.6
  61.5 0.0 copy-done.1
  61.5 0.0 copy-done.4
  61.5 2.2 %pick_own_rows.1 = (bf16[1152,384]{1,0:T(8,128)(2,1)S(1)}, f32[384,640]{1,0:T(8,128)S(1)}) custom-call(s32[1]{0:T(128)} %bitcast.tile_ref, s32[6]{0:T(128)S(1)} %copy-done.4, s32[1,768]{1,0:T(1,128)S(1)} %broadcast_in_dim.7.slots_ref, bf16[64,2,3456]{2,1,0:T(2,128)(2,1)S(1)} %all_to_all.10.own_ref, f32[3,1152]{1,0:T(4,128)S(1)} %copy-done.1), custom_call_target="tpu_custom_call" | custom-call | tf_op jit(solution)/shard_map/pick_own_rows/pallas_call | solution.py:296
  63.7 0.0 collective-permute-done.1.other_ref
  63.7 1.1 %mix_rows.1 = bf16[64,2,1920]{2,1,0:T(2,128)(2,1)S(1)} custom-call(s32[1]{0:T(128)} %bitcast.tile_ref, bf16[64,2,3456]{2,1,0:T(2,128)(2,1)S(1)} %collective-permute-done.1.other_ref, bf16[1152,384]{1,0:T(8,128)(2,1)S(1)} %get-tuple-element.17.other_hit, f32[384,640]{1,0:T(8,128)S(1)} %get-tuple-element.18.own_mixed, f32[3,1152]{1,0:T(4,128)S(1)} %copy-done.1), custom_call_target="tpu_custom_call" | custom-call | tf_op jit(solution)/shard_map/mix_rows/pallas_call | solution.py:327
  64.8 16.5 %all_to_all.11.own_ref = bf16[64,2,1920]{2,1,0:T(2,128)(2,1)S(1)} all-to-all(bf16[64,2,1920]{2,1,0:T(2,128)(2,1)S(1)} %mix_rows.1), channel_id=1, replica_groups=mesh['frame'=64,'tile'=2] {'frame'}, dimensions={0} | all-to-all | bytes 983040 | tf_op jit(solution)/shard_map/all_to_all | solution.py:431
  81.3 1.7 %collective-permute-start.2 = (bf16[64,2,1920]{2,1,0:T(2,128)(2,1)S(1)}, bf16[64,2,1920]{2,1,0:T(2,128)(2,1)S(1)}, u32[]{:S(2)}, u32[]{:S(2)}) collective-permute-start(bf16[64,2,1920]{2,1,0:T(2,128)(2,1)S(1)} %all_to_all.11.own_ref), channel_id=1, source_target_pairs={{0,1},{1,0},{2,3},{3,2},{4,5},{5,4},{6,7},{7,6},{8,9},{9,8},{10,11... | collective-permute-start | bytes 1474568 | tf_op jit(solution)/shard_map/ppermute | solution.py:432
  83.0 0.0 copy-done
  83.0 1.5 %project_own_channels.1.part_ref = f32[384,1792]{1,0:T(8,128)S(1)} custom-call(s32[1]{0:T(128)} %bitcast.tile_ref, bf16[64,2,1920]{2,1,0:T(2,128)(2,1)S(1)} %all_to_all.11.own_ref, bf16[1152,1792]{1,0:T(8,128)(2,1)S(1)} %copy-done), custom_call_target="tpu_custom_call" | custom-call | tf_op jit(solution)/shard_map/project_own_channels/pallas_call | solution.py:360
  84.4 0.0 collective-permute-done.2.other_ref
  84.5 1.9 %project_rows.1 = bf16[6,64,1792]{2,1,0:T(8,128)(2,1)} custom-call(s32[1]{0:T(128)} %bitcast.tile_ref, bf16[64,2,1920]{2,1,0:T(2,128)(2,1)S(1)} %collective-permute-done.2.other_ref, f32[384,1792]{1,0:T(8,128)S(1)} %project_own_channels.1.part_ref, bf16[1152,1792]{1,0:T(8,128)(2,1)S(1)} %copy-done), custom_call_target="tpu_custom_call" | custom-call | tf_op jit(solution)/shard_map/project_rows/pallas_call | solution.py:396
  (1 shorter events, 0.0 us)
Async XLA Ops:
  0.0 3.0 %copy-start.2 = (f32[1152]{0:T(1024)S(1)}, f32[1152]{0:T(1024)}, u32[]{:S(2)}) copy-start(f32[1152]{0:T(1024)} %gain_ref.3) | copy-start | bytes 13828
  0.0 3.0 %copy-start.3 = (f32[1152]{0:T(1024)S(1)}, f32[1152]{0:T(1024)}, u32[]{:S(2)}) copy-start(f32[1152]{0:T(1024)} %bias_ref.3) | copy-start | bytes 13828
  0.0 3.0 %copy-start.5 = (s32[64]{0:T(128)S(1)}, s32[64]{0:T(128)}, u32[]{:S(2)}) copy-start(s32[64]{0:T(128)} %param.19) | copy-start | bytes 772
  1.5 5.4 %collective-permute-start = (bf16[6,128,1152]{2,1,0:T(8,128)(2,1)S(1)}, bf16[6,128,1152]{2,1,0:T(8,128)(2,1)S(1)}, u32[]{:S(2)}, u32[]{:S(2)}) collective-permute-start(bf16[6,128,1152]{2,1,0:T(8,128)(2,1)S(1)} %cut_sent_half.1), channel_id=1, source_target_pairs={{0,1},{1,0},{2,3},{3,2},{4,5},{5,4},{6,7},{7,6},{8,9},{9,8},{10,11... | collective-permute-start | bytes 5308424 | tf_op jit(solution)/shard_map/ppermute | solution.py:419
  6.9 54.6 %copy-start.6 = (s32[768]{0:T(1024)S(1)}, s32[768]{0:T(1024)}, u32[]{:S(2)}) copy-start(s32[768]{0:T(1024)} %param.18) | copy-start | bytes 9220
  6.9 54.6 %copy-start.1 = (f32[3,1152]{1,0:T(4,128)S(1)}, f32[3,1152]{1,0:T(4,128)}, u32[]{:S(2)}) copy-start(f32[3,1152]{1,0:T(4,128)} %taps_ref.3) | copy-start | bytes 41476
  6.9 54.6 %copy-start.4 = (s32[6]{0:T(128)S(1)}, s32[6]{0:T(128)}, u32[]{:S(2)}) copy-start(s32[6]{0:T(128)} %lengths_ref.1) | copy-start | bytes 76
  59.9 23.1 %copy-start = (bf16[1152,1792]{1,0:T(8,128)(2,1)S(1)}, bf16[1152,1792]{1,0:T(8,128)(2,1)}, u32[]{:S(2)}) copy-start(bf16[1152,1792]{1,0:T(8,128)(2,1)} %w_ref.3) | copy-start | bytes 12386308
  59.9 3.8 %collective-permute-start.1 = (bf16[64,2,3456]{2,1,0:T(2,128)(2,1)S(1)}, bf16[64,2,3456]{2,1,0:T(2,128)(2,1)S(1)}, u32[]{:S(2)}, u32[]{:S(2)}) collective-permute-start(bf16[64,2,3456]{2,1,0:T(2,128)(2,1)S(1)} %all_to_all.10.own_ref), channel_id=1, source_target_pairs={{0,1},{1,0},{2,3},{3,2},{4,5},{5,4},{6,7},{7,6},{8,9},{9,8},{10,11... | collective-permute-start | bytes 2654216 | tf_op jit(solution)/shard_map/ppermute | solution.py:428
  81.3 3.1 %collective-permute-start.2 = (bf16[64,2,1920]{2,1,0:T(2,128)(2,1)S(1)}, bf16[64,2,1920]{2,1,0:T(2,128)(2,1)S(1)}, u32[]{:S(2)}, u32[]{:S(2)}) collective-permute-start(bf16[64,2,1920]{2,1,0:T(2,128)(2,1)S(1)} %all_to_all.11.own_ref), channel_id=1, source_target_pairs={{0,1},{1,0},{2,3},{3,2},{4,5},{5,4},{6,7},{7,6},{8,9},{9,8},{10,11... | collective-permute-start | bytes 1474568 | tf_op jit(solution)/shard_map/ppermute | solution.py:432
